TPU v7x, 32 devices: a whole 2x2x4 slice. The times are simulated.
32 devices in a mesh: lon: 8 (over y, x, core), dep: 4 (over z).
Axes of the slice: x: 2, y: 2, z: 4, core: 2. Of those that a mesh axis runs over, the one named last changes fastest.
Arguments:
- tracers: float32 [2, 80, 64, 1024], P(None, 'dep', None, 'lon'), may hold values from -6 to 6
- u_east: float32 [80, 64, 1024], P('dep', None, 'lon'), may hold values from -0.24 to 0.24
- v_north: float32 [80, 64, 1024], P('dep', None, 'lon'), may hold values from -0.24 to 0.24
- kappa_h: float32 [80, 64, 1024], P('dep', None, 'lon'), may hold values from 0.05 to 0.25
- kappa_v: float32 [80, 64, 1024], P('dep', None, 'lon'), may hold values from 0.3 to 300
- bottom: int32 [64, 1024], P(None, 'lon'), may hold values from 0 to 80
Outputs:
- tracers_out: float32 [2, 80, 64, 1024], P(None, 'dep', None, 'lon')
Inputs may be any that keep to these rules, and one draw needn't show every extreme that they name: Levels from bottom down are land; a column with 0 is all land.
All inputs are finite; a program needn't handle non-finite values.
Results may differ from a plain program's by a relative error of at most 0.0003.
Values sent between devices are 32-bit elements; how exact they have to be, the bound alone decides.
No kernel may reach another device: no remote copies, remote signals or barrier semaphores. Data moves between devices by JAX's collectives and lax.ppermute only.
A program may use at most 128 MiB of HBM per device.

v0:
```python
import functools

import jax
import jax.numpy as jnp
from jax import lax
from jax.experimental import pallas as pl
from jax.experimental.pallas import tpu as pltpu
from jax.sharding import PartitionSpec as P

SUB = 4
THERMAL = 0.2
HALINE = 0.8
GROUPS = 4
ROWS = 32
STRIP = 32
HUGE = 1e30
MIB = 1024 * 1024

VMEM = pl.BlockSpec(memory_space=pltpu.VMEM)
HBM = pl.BlockSpec(memory_space=pltpu.HBM)


def lane_ids(rows):
    return lax.broadcasted_iota(jnp.int32, (rows, 128), 1)


def roll_lanes(x, amount):
    amount = amount % 128
    return x if amount == 0 else pltpu.roll(x, amount, 1)


def shift_north(x):
    return jnp.concatenate([x[8:], pltpu.roll(x[:8], 7, 0)], axis=0)


def shift_south(x):
    return jnp.concatenate([pltpu.roll(x[-8:], 1, 0), x[:-8]], axis=0)


def rows_of(ref, v, *lead):
    return ref[(*lead, pl.ds(v, 8, ref.shape[-2] // 8), slice(None))]


def neighbours(regs, v):
    north = regs[v + 1] if v + 1 < len(regs) else pltpu.roll(regs[0], 7, 0)
    south = regs[v - 1] if v > 0 else pltpu.roll(regs[-1], 1, 0)
    return north, south


def slab_of(ref, *lead):
    return jnp.concatenate([rows_of(ref, v, *lead) for v in range(ref.shape[-2] // 8)], axis=0)


def call(body, out_shape, scratch, args, flops, in_bytes, limit, in_specs=None, out_specs=None):
    return pl.pallas_call(
        body,
        out_shape=out_shape,
        in_specs=in_specs or [VMEM] * len(args),
        out_specs=out_specs or jax.tree.map(lambda _: VMEM, out_shape),
        scratch_shapes=scratch,
        compiler_params=pltpu.CompilerParams(vmem_limit_bytes=int(limit * MIB)),
        cost_estimate=pl.CostEstimate(flops=flops, bytes_accessed=in_bytes, transcendentals=0),
    )(*args)


def f32(*shape):
    return jax.ShapeDtypeStruct(shape, jnp.float32)


def pack_kernel(
    t_hbm, u_hbm, v_hbm, kh_hbm, b_hbm,
    sw_ref, se_ref, bp_ref, ww_ref, we_ref, t0_ref, t1_ref, u_ref, v_ref, khb_ref,
    kh_buf, b_buf, first_buf, sems, more_sems,
):
    rows_e = u_ref.shape[0] // GROUPS
    lat = u_ref.shape[1]
    lane = lane_ids(lat)
    fields = ((t_hbm.at[0], t0_ref), (t_hbm.at[1], t1_ref), (u_hbm, u_ref), (v_hbm, v_ref))
    groups = [
        [
            pltpu.make_async_copy(
                src.at[pl.ds(g * rows_e, rows_e)], dst.at[pl.ds(g * rows_e, rows_e)], sems.at[g, n]
            )
            for n, (src, dst) in enumerate(fields)
        ]
        for g in range(GROUPS)
    ]
    tail = [
        pltpu.make_async_copy(b_hbm, b_buf, more_sems.at[0]),
        pltpu.make_async_copy(kh_hbm, kh_buf, more_sems.at[1]),
    ]
    for copy in sum(groups, []) + tail:
        copy.start()
    for g in range(GROUPS):
        for copy in groups[g]:
            copy.wait()
        for batch in (range(0, rows_e // 2), range(rows_e // 2, rows_e)):
            rolled = {
                (r, f): roll_lanes(slab_of(ref, g * rows_e + r), STRIP * g + 8 * f)
                for r in batch
                for f, ref in enumerate((t0_ref, t1_ref, u_ref, v_ref))
            }
            done = []
            for r in batch:
                low = rolled[r, 0]
                high = None
                if g > 0:
                    low = jnp.where(lane >= STRIP * g, low, sw_ref[r])
                    high = jnp.where(lane >= STRIP * g - 8, rolled[r, 0], se_ref[r])
                for f in range(1, 4):
                    start = STRIP * g + 8 * f
                    low = jnp.where(lane >= start, rolled[r, f], low)
                    if high is None:
                        high = rolled[r, f]
                    else:
                        high = jnp.where(lane >= start - 8, rolled[r, f], high)
                if g == GROUPS - 1:
                    high = jnp.where(lane >= 120, first_buf[r], high)
                done.append((r, low, high))
            for r, low, high in done:
                if g == 0:
                    first_buf[r] = rolled[r, 0]
                sw_ref[r] = low
                se_ref[r] = high
    for copy in tail:
        copy.wait()
    bottom = slab_of(b_buf).astype(jnp.float32)
    place = bottom
    for g in range(1, GROUPS):
        place = jnp.where(lane >= STRIP * g - 8, roll_lanes(bottom, STRIP * g), place)
    place = jnp.where(lane >= 120, bottom, place)
    bp_ref[...] = place

    def kappa(r):
        out = None
        for g in range(GROUPS):
            rolled = roll_lanes(slab_of(kh_buf, g * rows_e + r), STRIP * g + 23)
            out = rolled if g == 0 else jnp.where(lane >= STRIP * g + 8, rolled, out)
        return out

    khb_ref[0] = slab_of(kh_buf, 0)
    khb_ref[1] = slab_of(kh_buf, GROUPS * rows_e - 1)
    last = rows_e - 1
    kappa_last = kappa(last)
    lane_q = lane % STRIP
    low_last, high_last = sw_ref[last], se_ref[last]
    wires = []
    for r in range(last):
        k = kappa(r)
        low, high = sw_ref[r], se_ref[r]
        west = (low, roll_lanes(low, -2), roll_lanes(low, -4), roll_lanes(low, -6), k)
        east = (
            roll_lanes(high, 6), roll_lanes(high, 4), roll_lanes(high, 2), roll_lanes(high, -1),
            roll_lanes(k, 1),
        )
        west += (roll_lanes(low_last, 24 - 8 * r),)
        east += (roll_lanes(high_last, 5 if r == 3 else 30 - 8 * r),)
        if r == 3:
            west += (roll_lanes(kappa_last, 6),)
            east += (roll_lanes(kappa_last, 7),)
        else:
            west += (roll_lanes(place, 30 - 2 * r),)
            east += (roll_lanes(place, 36 - 2 * r),)
        starts = (6, 12, 18, 23, 24, 29 if r == 3 else 30)
        for ref, parts in ((ww_ref, west), (we_ref, east)):
            wire = parts[0]
            for start, part in zip(starts, parts[1:]):
                wire = jnp.where(lane_q >= start, part, wire)
            wires.append((ref, r, wire))
    for ref, r, wire in wires:
        ref[r] = wire


def advect_block(slabs, get_c, get_u, get_v, get_level, bx, by, buf, coef, put):
    regs = bx.shape[0] // 8
    for i, slab in enumerate(slabs):
        level = get_level(slab)
        um = jnp.where(level < bx, get_u(slab), 0.0)
        vm = jnp.where(level < by, get_v(slab), 0.0)
        uw = roll_lanes(um, 1)
        vs = shift_south(vm)
        coef[0, i] = (
            1.0
            - jnp.maximum(um, 0.0)
            + jnp.minimum(uw, 0.0)
            - jnp.maximum(vm, 0.0)
            + jnp.minimum(vs, 0.0)
        )
        coef[1, i] = -jnp.minimum(um, 0.0)
        coef[2, i] = jnp.maximum(uw, 0.0)
        coef[3, i] = -jnp.minimum(vm, 0.0)
        coef[4, i] = jnp.maximum(vs, 0.0)
        for tr in range(2):
            buf[0, 2 * i + tr] = get_c(tr, slab)
    for step in range(SUB):
        src, dst = step % 2, (step + 1) % 2
        for i, slab in enumerate(slabs):
            now = [
                [buf[src, 2 * i + tr, 8 * v : 8 * v + 8] for v in range(regs)] for tr in range(2)
            ]
            for v in range(regs):
                js = slice(8 * v, 8 * v + 8)
                a, b, c, d, e = (coef[n, i, js] for n in range(5))
                for tr in range(2):
                    here = now[tr][v]
                    north, south = neighbours(now[tr], v)
                    new = (
                        a * here
                        + b * roll_lanes(here, -1)
                        + c * roll_lanes(here, 1)
                        + d * north
                        + e * south
                    )
                    if step < SUB - 1:
                        buf[dst, 2 * i + tr, js] = new
                    else:
                        put(tr, slab, js, new)


def face_limits(bottom):
    lat = bottom.shape[0]
    rows = lax.broadcasted_iota(jnp.int32, bottom.shape, 0)
    north = jnp.where(rows == lat - 1, 0.0, shift_north(bottom))
    return jnp.minimum(bottom, roll_lanes(bottom, -1)), jnp.minimum(bottom, north)


def lat_limits(bottom):
    lat = bottom.shape[0]
    rows = lax.broadcasted_iota(jnp.int32, bottom.shape, 0)
    north = jnp.where(rows == lat - 1, 0.0, shift_north(bottom))
    south = jnp.where(rows == 0, 0.0, shift_south(bottom))
    return jnp.minimum(north, south)


def advect_kernel(start, t0_ref, t1_ref, u_ref, v_ref, b_ref, earlier_ref, out_ref, buf, coef):
    del earlier_ref
    count, lat = out_ref.shape[1], out_ref.shape[2]
    base = lax.axis_index("dep") * t0_ref.shape[0] + start
    bx, by = face_limits(slab_of(b_ref).astype(jnp.float32))

    def put(tr, slab, js, new):
        out_ref[tr, slab, js] = new

    advect_block(
        list(range(count)),
        lambda tr, s: slab_of((t0_ref, t1_ref)[tr], start + s),
        lambda s: slab_of(u_ref, start + s),
        lambda s: slab_of(v_ref, start + s),
        lambda s: (base + s).astype(jnp.float32),
        bx,
        by,
        buf,
        coef,
        put,
    )


def join(lane_q, own, east, west):
    halo = jnp.where(lane_q < 16, east, west)
    return jnp.where((lane_q >= 8) & (lane_q < 24), halo, own)


def west_patch(slab, g):
    return roll_lanes(slab, -(STRIP * g + 24))


def east_patch(slab, g):
    return roll_lanes(slab, 120 - STRIP * g)


def patched(main, slab, g, lane):
    return jnp.where(
        lane < 4, west_patch(slab, g), jnp.where(lane >= 124, east_patch(slab, g), main)
    )


def own_kernel(sw_ref, se_ref, bp_ref, earlier_ref, own_ref, ownb_ref):
    del earlier_ref
    rows_e, lat = sw_ref.shape[0], sw_ref.shape[1]
    lane_q = lane_ids(lat) % STRIP
    for r in range(rows_e):
        made = [
            jnp.where(
                lane_q < 16, roll_lanes(se_ref[r], 8 - 8 * f), roll_lanes(sw_ref[r], 24 - 8 * f)
            )
            for f in range(4)
        ]
        for f in range(4):
            own_ref[f, r] = made[f]
    place = bp_ref[...]
    ownb_ref[...] = jnp.where(lane_q < 16, roll_lanes(place, 8), roll_lanes(place, 24))


def pair_response(abc_ref, pair_ref, me):
    upper = lax.rem(me, 2) == 0
    low_pair = me < 2
    inv_t = 1.0 / (pair_ref[0] + jnp.where(upper, abc_ref[1], abc_ref[0]))
    c_pair = jnp.where(upper == low_pair, pair_ref[1], abc_ref[2])
    share = c_pair * inv_t
    return share, inv_t, jnp.where(upper, abc_ref[0], abc_ref[1]) - c_pair * share


def fold_strip(slab, place):
    lane = lane_ids(8)
    folded = jnp.zeros((8, 128), jnp.float32)
    for v in range(slab.shape[0] // 8):
        rolled = roll_lanes(slab[8 * v : 8 * v + 8], 16 * v - place)
        folded = jnp.where(lane >= 16 * v, rolled, folded)
    return folded


def unfold_strip(folded, place, regs):
    return jnp.concatenate([roll_lanes(folded, place - 16 * v) for v in range(regs)], axis=0)


def edge_kernel(
    own_ref, ownb_ref, re_ref, rw_ref, b_ref, north_half, south_half, kh_ref, abc_ref, pair_ref,
    ea_ref, ek_ref, eb_ref, bmx_ref, first_ref, second_ref, red_ref,
    buf, coef, fields, pay,
):
    levels, lat = kh_ref.shape[0], kh_ref.shape[1]
    rows_e = levels // GROUPS
    me = lax.axis_index("dep")
    base = me * levels
    parity = lax.rem(me, 2)
    up_ref, down_ref = pay.at[1 - parity], pay.at[parity]
    lane = lane_ids(lat)
    lane_q = lane % STRIP
    bottom = slab_of(b_ref).astype(jnp.float32)
    east = [roll_lanes(re_ref[r], 2 * r - 22) for r in range(3)]
    west = [roll_lanes(rw_ref[r], 2 * r - 12) for r in range(3)]
    eb = join(
        lane_q,
        ownb_ref[...],
        jnp.where(lane_q < 10, east[0], jnp.where(lane_q < 12, east[1], east[2])),
        jnp.where(lane_q < 20, west[0], jnp.where(lane_q < 22, west[1], west[2])),
    )
    eb_ref[...] = eb
    b_west = roll_lanes(jnp.where(lane == 127, west_patch(eb, 0), bottom), 1)
    b_east = roll_lanes(jnp.where(lane == 0, east_patch(eb, 0), bottom), -1)
    bmx_ref[...] = jnp.minimum(b_west, b_east)
    last = rows_e - 1
    for r in range(rows_e):
        at, shift_e, shift_w = (3, -21, -6) if r == last else (r, -15, 0)
        ek_ref[r] = jnp.where(
            lane_q < 16, roll_lanes(re_ref[at], shift_e), roll_lanes(rw_ref[at], shift_w)
        )
        made = []
        for f in range(4):
            at, start = (f, 24) if r == last else (r, 6 * f)
            made.append(
                join(
                    lane_q,
                    own_ref[f, r],
                    roll_lanes(re_ref[at], 8 - start),
                    roll_lanes(rw_ref[at], (19 if f == 3 else 18) - start),
                )
            )
        for f in range(4):
            fields[f, r] = made[f]
    bx, by = face_limits(eb)
    level0 = (base + (lane // STRIP) * rows_e).astype(jnp.float32)

    def put(tr, slab, js, new):
        ea_ref[tr, slab, js] = new

    advect_block(
        list(range(rows_e)),
        lambda tr, s: fields[tr, s],
        lambda s: fields[2, s],
        lambda s: fields[3, s],
        lambda s: level0 + float(s),
        bx,
        by,
        buf,
        coef,
        put,
    )
    top, half = rows_e - 1, levels // 2
    for tr in range(2):
        for n, (k, slab) in enumerate(((0, ea_ref[tr, 0]), (1, ea_ref[tr, 1]))):
            at = (2 * n + tr) * lat
            up_ref[at : at + lat] = patched(north_half[tr, k], slab, 0, lane)
        for n, (k, slab) in enumerate(
            ((half - 1, ea_ref[tr, top]), (half - 2, ea_ref[tr, top - 1]))
        ):
            at = (2 * n + tr) * lat
            down_ref[at : at + lat] = patched(south_half[tr, k], slab, 3, lane)
        at = 4 * lat + 8 * tr
        up_ref[at : at + 8] = fold_strip(ea_ref[tr, 0], 8)
        down_ref[at : at + 8] = fold_strip(ea_ref[tr, top], 3 * STRIP + 8)
    up_ref[4 * lat + 16 : 5 * lat + 16] = slab_of(kh_ref, 0)
    down_ref[4 * lat + 16 : 5 * lat + 16] = slab_of(kh_ref, levels - 1)
    first_ref[...] = pay[0, 0 : 4 * lat + 16]
    second_ref[0 : 5 * lat + 16] = pay[1]
    response = pair_response(abc_ref, pair_ref, me)
    for n in range(3):
        red_ref[n] = response[n]
    second_ref[5 * lat + 16 : 6 * lat + 16] = response[2]


def slopes(gx, gy, gz):
    rx, ry, rz = (-0.5 * THERMAL * g[0] + 0.5 * HALINE * g[1] for g in (gx, gy, gz))
    scale = rz / (1.0 + rx * rx + ry * ry + rz * rz)
    return rx * scale, ry * scale


def flux_xyz(gx, gy, gz, kappa, need_xy=True):
    sx, sy = slopes(gx, gy, gz)
    kx, ky = kappa * sx, kappa * sy
    kz = kx * sx + ky * sy
    fz = [kx * gx[n] + ky * gy[n] + kz * gz[n] for n in range(2)]
    if not need_xy:
        return None, None, fz
    fx = [kappa * gx[n] + kx * gz[n] for n in range(2)]
    fy = [kappa * gy[n] + ky * gz[n] for n in range(2)]
    return fx, fy, fz


def flux_x_edge(gx, gy, gz, kappa):
    sx, _ = slopes(gx, gy, gz)
    kx = kappa * sx
    return [kappa * gx[n] + kx * gz[n] for n in range(2)]


def diff(mask, high, low):
    return jnp.where(mask, high - low, 0.0)


def edge_flux_row(r, rows, ek, eb, ebx, eby, level0):
    level = level0 + r
    mx = level < ebx
    my = level < eby
    mz = (level + 1.0 < eb) & (level >= 1.0)
    kappa = jnp.where((level < eb) & (level >= 0.0), 0.25 * ek, 0.0)
    gx, gy, gz = [], [], []
    for tr in range(2):
        here = rows[tr, r + 1]
        gx.append(diff(mx, roll_lanes(here, -1), roll_lanes(here, 1)))
        gy.append(diff(my, shift_north(here), shift_south(here)))
        gz.append(diff(mz, rows[tr, r + 2], rows[tr, r]))
    return flux_x_edge(gx, gy, gz, kappa)


def edge_limits(eb):
    return (
        jnp.minimum(roll_lanes(eb, 1), roll_lanes(eb, -1)),
        lat_limits(eb),
    )


def zonal_change(fx, west, east, lane):
    return roll_lanes(jnp.where(lane == 0, east, fx), -1) - roll_lanes(
        jnp.where(lane == 127, west, fx), 1
    )


def divergence(fx, fy, slab, g, lane):
    return zonal_change(fx, west_patch(slab, g), east_patch(slab, g), lane) + (
        shift_north(fy) - shift_south(fy)
    )


def patch_kernel(
    north_half, south_half, ea_ref, ek_ref, eb_ref,
    full_ref, gx_ref, efx_ref,
    rows,
):
    levels, lat = full_ref.shape[1], full_ref.shape[2]
    rows_e = levels // GROUPS
    base = lax.axis_index("dep") * levels
    lane = lane_ids(lat)
    eb = eb_ref[...]
    ebx, eby = edge_limits(eb)
    level0 = (base + (lane // STRIP) * rows_e).astype(jnp.float32)
    for tr in range(2):
        for r in range(rows_e):
            rows[tr, r + 1] = ea_ref[tr, r]
        rows[tr, 0] = roll_lanes(ea_ref[tr, rows_e - 1], STRIP)
        rows[tr, rows_e + 1] = roll_lanes(ea_ref[tr, 0], -STRIP)
    found = [
        edge_flux_row(r, rows, ek_ref[r], eb, ebx, eby, level0) for r in range(rows_e)
    ]
    for r in range(rows_e):
        for tr in range(2):
            efx_ref[tr, r] = found[r][tr]

    lane = lane_ids(ROWS)
    units = [(g, slice(j, j + ROWS)) for g in range(GROUPS) for j in range(0, lat, ROWS)]

    def patch(r, _):
        def fetch(unit):
            g, js = unit
            strips = [ea_ref[tr, r, js] for tr in range(2)]
            half = (north_half, south_half)[2 * g // GROUPS]
            mains = [half[tr, g % (GROUPS // 2) * rows_e + r, js] for tr in range(2)]
            return [(west_patch(x, g), east_patch(x, g), y) for x, y in zip(strips, mains)]

        def put(unit, mains, rolled):
            g, js = unit
            for tr in range(2):
                full_ref[tr, g * rows_e + r, js] = mains[tr]
                gx_ref[tr, g * rows_e + r, js] = rolled[tr][0] - rolled[tr][1]

        waiting = None
        fetched = fetch(units[0])
        for n, unit in enumerate(units):
            now = fetched
            fetched = fetch(units[n + 1]) if n + 1 < len(units) else None
            mains, rolled = [], []
            for west, east, main in now:
                main = jnp.where(lane < 4, west, jnp.where(lane >= 124, east, main))
                mains.append(main)
                rolled.append(
                    (
                        roll_lanes(jnp.where(lane == 0, east, main), -1),
                        roll_lanes(jnp.where(lane == 127, west, main), 1),
                    )
                )
            if waiting is not None:
                put(*waiting)
            waiting = (unit, mains, rolled)
        put(*waiting)
        return 0

    lax.fori_loop(0, rows_e, patch, 0)


def flux_kernel(
    full_ref, gx_ref, efx_ref, bmx_ref, b_ref, kh_ref,
    q_ref, fz_ref,
    limits,
):
    levels, lat = full_ref.shape[1], full_ref.shape[2]
    rows_e = levels // GROUPS
    base = lax.axis_index("dep") * levels
    lane = lane_ids(lat)
    bottom = slab_of(b_ref).astype(jnp.float32)
    limits[0] = bmx_ref[...]
    limits[1] = lat_limits(bottom)
    limits[2] = bottom

    def north_rows(tr, k, j):
        if j + 8 + ROWS <= lat:
            return full_ref[tr, k, j + 8 : j + 8 + ROWS]
        return jnp.concatenate(
            [full_ref[tr, k, j + 8 : lat], pltpu.roll(full_ref[tr, k, 0:8], 7, 0)], axis=0
        )

    def south_rows(tr, k, j):
        if j >= 8:
            return full_ref[tr, k, j - 8 : j - 8 + ROWS]
        return jnp.concatenate(
            [pltpu.roll(full_ref[tr, k, lat - 8 : lat], 1, 0), full_ref[tr, k, 0 : ROWS - 8]],
            axis=0,
        )

    def fluxes(r, _):
        for g in range(GROUPS):
            k = g * rows_e + r
            above, below = jnp.maximum(k - 1, 0), jnp.minimum(k + 1, levels - 1)
            level = (base + k).astype(jnp.float32)
            level_z = jnp.where(level >= 1.0, level + 1.0, HUGE)
            sides = [
                (west_patch(efx_ref[tr, r], g), east_patch(efx_ref[tr, r], g)) for tr in range(2)
            ]
            fxs, fys, fzs = [[], []], [[], []], [[], []]
            for j in range(0, lat, ROWS):
                js = slice(j, j + ROWS)
                mx = level < limits[0, js]
                my = level < limits[1, js]
                mz = level_z < limits[2, js]
                kh = jnp.concatenate(
                    [rows_of(kh_ref, v, k) for v in range(j // 8, (j + ROWS) // 8)], axis=0
                )
                kappa = jnp.where(level < limits[2, js], 0.25 * kh, 0.0)
                gx, gy, gz = [], [], []
                for tr in range(2):
                    gx.append(jnp.where(mx, gx_ref[tr, k, js], 0.0))
                    gy.append(diff(my, north_rows(tr, k, j), south_rows(tr, k, j)))
                    gz.append(diff(mz, full_ref[tr, below, js], full_ref[tr, above, js]))
                fx, fy, fz = flux_xyz(gx, gy, gz, kappa)
                for tr in range(2):
                    fxs[tr].append(fx[tr])
                    fys[tr].append(fy[tr])
                    fzs[tr].append(fz[tr])
            wet = level < limits[2]
            new = []
            for tr in range(2):
                fy = jnp.concatenate(fys[tr], axis=0)
                change = zonal_change(jnp.concatenate(fxs[tr], axis=0), *sides[tr], lane)
                change = change + (shift_north(fy) - shift_south(fy))
                new.append(full_ref[tr, k] + jnp.where(wet, change, 0.0))
            for tr in range(2):
                q_ref[tr, k] = new[tr]
                fz_ref[tr, k] = jnp.concatenate(fzs[tr], axis=0)
        return 0

    lax.fori_loop(0, rows_e, fluxes, 0)


def factor_kernel(
    kv_ref, b_ref, khb_ref, inv_ref, ei_ref, ratio_ref, a_ref, bb_ref, abc_ref, msg_ref
):
    levels, lat = kv_ref.shape[0], kv_ref.shape[1]
    base = lax.axis_index("dep") * levels
    bottom = slab_of(b_ref).astype(jnp.float32)

    def coupling(k):
        level = (base + k).astype(jnp.float32)
        level = jnp.where(level >= 1.0, level, HUGE)
        return jnp.where(level < bottom, slab_of(kv_ref, k), 0.0)

    top = coupling(0)
    e = jnp.zeros((lat, 128), jnp.float32)
    q = e
    za = jnp.ones((lat, 128), jnp.float32)
    for k in range(levels):
        low = coupling(k + 1) if k + 1 < levels else jnp.zeros((lat, 128), jnp.float32)
        eq = 1.0 + e * q
        inv = 1.0 / (eq + low)
        inv_ref[k] = inv
        ei = e * inv
        ei_ref[k] = ei
        ratio_ref[k] = low * inv
        za = inv if k == 0 else za * ei
        a_ref[k] = za
        q = eq * inv
        e = low
    bb_ref[levels - 1] = inv
    b = inv
    a = za
    for k in range(levels - 2, -1, -1):
        ratio = ratio_ref[k]
        b = ratio * b
        a = a_ref[k] + ratio * a
        bb_ref[k] = b
        a_ref[k] = a
    a = a + jnp.where(top > 0.0, 1.0 / jnp.maximum(top, 1e-30), HUGE)
    abc_ref[0] = a
    abc_ref[1] = inv
    abc_ref[2] = b
    upper = lax.rem(lax.axis_index("dep"), 2) == 0
    msg_ref[0] = jnp.where(upper, inv, a)
    msg_ref[1] = b
    msg_ref[2] = jnp.where(upper, khb_ref[1], khb_ref[0])


def solve_kernel(
    full_ref, q_ref, fz_ref, ea_ref, ek_ref, eb_ref, bmx_ref, b_ref, kh_ref,
    first_ref, second_ref, inv_ref, ei_ref, ratio_ref, red_ref, pair_ref,
    y_ref, m3_ref, m2_ref, m1_ref, both_ref, own_ref,
    pad, epad, fze, halo,
):
    levels, lat = q_ref.shape[1], q_ref.shape[2]
    rows_e = levels // GROUPS
    last = levels - 1
    top = rows_e - 1
    me = lax.axis_index("dep")
    base = me * levels
    parity = lax.rem(me, 2)
    outer = (me == 0) | (me == 3)
    upper = parity == 0
    sign = jnp.where(me < 2, 1.0, -1.0)
    lane = lane_ids(lat)
    halo[0, 0 : 4 * lat + 16] = first_ref[...]
    halo[0, 4 * lat + 16 : 5 * lat + 16] = pair_ref[2]
    halo[1] = second_ref[0 : 5 * lat + 16]
    above_ref, below_ref = halo.at[1 - parity], halo.at[parity]

    share = red_ref[0]
    both = red_ref[2] + second_ref[5 * lat + 16 : 6 * lat + 16]
    cross = share / both
    inside = red_ref[1] + share * cross
    for n, value in enumerate((share, red_ref[1], both)):
        own_ref[n] = value
    both_ref[...] = both

    eb = eb_ref[...]
    ebx, eby = edge_limits(eb)
    level0 = (base + (lane // STRIP) * rows_e).astype(jnp.float32)
    for tr in range(2):
        pad[tr, 0] = above_ref[(2 + tr) * lat : (3 + tr) * lat]
        pad[tr, 1] = above_ref[tr * lat : (1 + tr) * lat]
        for n, k in enumerate((0, 1, 2, last - 2, last - 1, last)):
            pad[tr, n + 2] = full_ref[tr, k]
        pad[tr, 8] = below_ref[tr * lat : (1 + tr) * lat]
        pad[tr, 9] = below_ref[(2 + tr) * lat : (3 + tr) * lat]
        for r in range(rows_e):
            epad[tr, r + 1] = ea_ref[tr, r]
        at = 4 * lat + 8 * tr
        corner_up = unfold_strip(above_ref[at : at + 8], 3 * STRIP + 8, lat // 8)
        corner_dn = unfold_strip(below_ref[at : at + 8], 8, lat // 8)
        epad[tr, 0] = roll_lanes(
            jnp.where(lane >= 3 * STRIP, corner_up, ea_ref[tr, top]), STRIP
        )
        epad[tr, rows_e + 1] = roll_lanes(
            jnp.where(lane < STRIP, corner_dn, ea_ref[tr, 0]), -STRIP
        )
    efx = {
        r + 1: edge_flux_row(r, epad, ek_ref[r], eb, ebx, eby, level0) for r in (0, top)
    }

    bottom = slab_of(b_ref).astype(jnp.float32)
    bmy = lat_limits(bottom)
    bmx = bmx_ref[...]
    ends = (
        (1, -1, 0, 0, above_ref[4 * lat + 16 : 5 * lat + 16], True),
        (2, 0, 1, 0, slab_of(kh_ref, 0), False),
        (7, last, top + 1, 3, slab_of(kh_ref, last), False),
        (8, last + 1, top + 2, 3, below_ref[4 * lat + 16 : 5 * lat + 16], True),
    )
    spread = {}
    for m, (n, k, er, g, kappa_slab, only_z) in enumerate(ends):
        level = (base + k).astype(jnp.float32)
        level_z = jnp.where(level >= 1.0, level + 1.0, HUGE)
        level_h = jnp.where(level >= 0.0, level, HUGE)
        mx = level_h < bmx
        my = level_h < bmy
        mz = level_z < bottom
        kappa = jnp.where(level_h < bottom, 0.25 * kappa_slab, 0.0)
        gx, gy, gz = [], [], []
        for tr in range(2):
            slab, main = epad[tr, er], pad[tr, n]
            change = zonal_change(main, west_patch(slab, g), east_patch(slab, g), lane)
            gx.append(jnp.where(mx, change, 0.0))
            gy.append(diff(my, shift_north(main), shift_south(main)))
            gz.append(diff(mz, pad[tr, n + 1], pad[tr, n - 1]))
        fx, fy, fz = flux_xyz(gx, gy, gz, kappa, not only_z)
        for tr in range(2):
            fze[tr, m] = fz[tr]
            if not only_z:
                spread[k, tr] = divergence(fx[tr], fy[tr], efx[er][tr], g, lane)

    def vertical_flux(tr, k):
        place = {-1: 0, 0: 1, last: 2, last + 1: 3}.get(k)
        return fz_ref[tr, k] if place is None else fze[tr, place]

    z = [None, None]
    for k in range(levels):
        level = (base + k).astype(jnp.float32)
        wet = level < bottom
        for tr in range(2):
            change = vertical_flux(tr, k + 1) - vertical_flux(tr, k - 1)
            if k == 0 or k == last:
                change = change + spread[k, tr]
                start = pad[tr, 2 if k == 0 else 7]
            else:
                start = q_ref[tr, k]
            rhs = start + jnp.where(wet, change, 0.0)
            new = rhs * inv_ref[k]
            z[tr] = new if k == 0 else new + ei_ref[k] * z[tr]
        for tr in range(2):
            y_ref[tr, k] = z[tr]
    low = list(z)
    for k in range(last - 1, -1, -1):
        ratio = ratio_ref[k]
        z = [y_ref[tr, k] + ratio * z[tr] for tr in range(2)]
        for tr in range(2):
            y_ref[tr, k] = z[tr]
    for tr in range(2):
        near = jnp.where(upper, low[tr], z[tr])
        far = jnp.where(upper, z[tr], low[tr])
        m1_ref[tr] = jnp.where(outer, near, sign * (inside * near - cross * far))
        value = jnp.where(outer, share * near, far - share * near)
        m2_ref[tr] = value
        m3_ref[tr] = value


def finish_kernel(
    y_ref, a_ref, bb_ref, own_ref, r3_ref, r2_ref, r1_ref, both_ref, out_hbm, out, sems
):
    levels = y_ref.shape[1]
    me = lax.axis_index("dep")
    upper = lax.rem(me, 2) == 0
    outer = (me == 0) | (me == 3)
    sign = jnp.where(me < 2, 1.0, -1.0)
    share, inv_t = own_ref[0], own_ref[1]
    inv_e = 1.0 / jnp.where(outer, both_ref[...], own_ref[2])
    cross = share * inv_e
    inside = inv_t + share * cross
    tops, lows = [], []
    for tr in range(2):
        y_top, y_low = y_ref[tr, 0], y_ref[tr, levels - 1]
        near = jnp.where(upper, y_low, y_top)
        far = jnp.where(upper, y_top, y_low)
        mate, across = r1_ref[tr], r2_ref[tr] + r3_ref[tr]
        pair_flux = jnp.where(
            outer,
            mate + sign * (cross * across - inside * near),
            sign * (inside * (near - mate) + cross * (across - far)),
        )
        middle = sign * (inv_e * (across - far + share * near) - cross * mate)
        middle = jnp.where(outer, 0.0, middle)
        tops.append(jnp.where(upper, middle, pair_flux))
        lows.append(jnp.where(upper, pair_flux, middle))
    step, regs = levels // GROUPS, y_ref.shape[2] // 8
    copies = []
    for part in range(GROUPS):
        for k in range(part * step, (part + 1) * step):
            a, b = a_ref[k], bb_ref[k]
            new = [y_ref[tr, k] - tops[tr] * a + lows[tr] * b for tr in range(2)]
            for tr in range(2):
                for v in range(regs):
                    out[tr, k, pl.ds(v, 8, regs), :] = new[tr][8 * v : 8 * v + 8]
        for tr in range(2):
            span = (tr, pl.ds(part * step, step))
            copies.append(
                pltpu.make_async_copy(out.at[span], out_hbm.at[span], sems.at[tr, part])
            )
            copies[-1].start()
    for copy in copies:
        copy.wait()


def per_device(tracers, u_east, v_north, kappa_h, kappa_v, bottom):
    _, levels, lat, lon = tracers.shape
    rows_e = levels // GROUPS
    lon_n, dep_n = lax.axis_size("lon"), lax.axis_size("dep")
    east = [(i, (i + 1) % lon_n) for i in range(lon_n)]
    west = [(t, s) for s, t in east]
    slab = lat * lon * 4
    slabs = lambda *lead: f32(*lead, lat, lon)
    work = lambda *lead: pltpu.VMEM(lead + (lat, lon), jnp.float32)

    with jax.named_scope("pack"):
        sw, se, bp, ww, we, t0, t1, u, v, khb = call(
            pack_kernel,
            (slabs(rows_e),) * 2 + (slabs(),) + (slabs(rows_e - 1),) * 2 + (slabs(levels),) * 4
            + (slabs(2),),
            [
                work(levels), pltpu.VMEM((lat, lon), jnp.int32), work(rows_e),
                pltpu.SemaphoreType.DMA((GROUPS, 4)), pltpu.SemaphoreType.DMA((2,)),
            ],
            (tracers, u_east, v_north, kappa_h, bottom), 10**6, 6 * levels * slab, 50.5,
            in_specs=[HBM] * 5,
        )
    with jax.named_scope("lon_halo"):
        r_east = lax.ppermute(ww, "lon", west)
        r_west = lax.ppermute(we, "lon", east)
    with jax.named_scope("factor"):
        inv, ei, ratio, a_end, b_end, abc, msg = call(
            factor_kernel, (slabs(levels),) * 5 + (slabs(3),) * 2, [],
            (kappa_v, bottom, khb), 10**7, 6 * levels * slab, 16,
        )
    swap = [(i, i ^ 1) for i in range(dep_n)]
    with jax.named_scope("pair_coefficients"):
        pair = lax.ppermute(msg, "dep", swap)
    half = levels // 2

    def advect_half(start, earlier):
        return call(
            functools.partial(advect_kernel, start), slabs(2, half),
            [work(2, 2 * half), work(5, half)],
            (t0, t1, u, v, bottom, earlier), 10**7, 4 * levels * slab, 16,
        )

    with jax.named_scope("advect_north"):
        north_half = advect_half(0, abc)
    with jax.named_scope("advect_south"):
        south_half = advect_half(half, abc)
    with jax.named_scope("own_strips"):
        own_strips, own_bottom = call(
            own_kernel, (slabs(4, rows_e), slabs()), [],
            (sw, se, bp, abc), 10**6, 8 * rows_e * slab, 16,
        )
    rows_pay = 5 * lat + 16
    with jax.named_scope("advect_edge"):
        ea, ek, eb, bmx, first, second, red = call(
            edge_kernel,
            (
                slabs(2, rows_e), slabs(rows_e), slabs(), slabs(),
                f32(rows_pay - lat, lon), f32(rows_pay + lat, lon), slabs(3),
            ),
            [
                work(2, 2 * rows_e), work(5, rows_e), work(4, rows_e),
                pltpu.VMEM((2, rows_pay, lon), jnp.float32),
            ],
            (own_strips, own_bottom, r_east, r_west, bottom, north_half, south_half, kappa_h, abc, pair),
            10**6, 3 * levels * slab, 16,
        )
    other = []
    for i in range(lon_n * dep_n):
        row, place = divmod(i, dep_n)
        if place in (0, dep_n - 1):
            other.append((i, (row ^ 1) * dep_n + place))
        else:
            other.append((i, i + 1 if place % 2 else i - 1))
    with jax.named_scope("dep_halo"):
        first = lax.ppermute(first, "dep", swap)
        second = lax.ppermute(second, ("lon", "dep"), other)
    with jax.named_scope("patch"):
        full, gx, efx = call(
            patch_kernel, (slabs(2, levels), slabs(2, levels), slabs(2, rows_e)),
            [work(2, rows_e + 2)],
            (north_half, south_half, ea, ek, eb), 10**7, 8 * levels * slab, 16,
        )
    with jax.named_scope("fluxes"):
        q_part, fz = call(
            flux_kernel, (slabs(2, levels), slabs(2, levels)), [work(3)],
            (full, gx, efx, bmx, bottom, kappa_h), 10**7, 10 * levels * slab, 16,
        )
    with jax.named_scope("solve"):
        y, m3, m2, m1, both, own = call(
            solve_kernel, (slabs(2, levels), slabs(2), slabs(2), slabs(2), slabs(), slabs(3)),
            [
                work(2, 10), work(2, rows_e + 2), work(2, 4),
                pltpu.VMEM((2, rows_pay, lon), jnp.float32),
            ],
            (
                full, q_part, fz, ea, ek, eb, bmx, bottom, kappa_h, first, second,
                inv, ei, ratio, red, pair,
            ),
            10**7, 12 * levels * slab, 24,
        )
    with jax.named_scope("interfaces"):
        m3 = lax.ppermute(m3, "dep", [(i, i ^ 3) for i in range(dep_n)])
        m2 = lax.ppermute(m2, "dep", [(i, i ^ 2) for i in range(dep_n)])
        m1 = lax.ppermute(m1, "dep", swap)
        both = lax.ppermute(both, "dep", swap)
    with jax.named_scope("finish"):
        return call(
            finish_kernel, slabs(2, levels),
            [work(2, levels), pltpu.SemaphoreType.DMA((2, GROUPS))],
            (y, a_end, b_end, own, m3, m2, m1, both), 10**6, 6 * levels * slab, 16,
            out_specs=HBM,
        )


def solution(mesh):
    in_specs = (
        P(None, "dep", None, "lon"),
        P("dep", None, "lon"),
        P("dep", None, "lon"),
        P("dep", None, "lon"),
        P("dep", None, "lon"),
        P(None, "lon"),
    )
    out_specs = P(None, "dep", None, "lon")
    return jax.shard_map(
        per_device, mesh=mesh, in_specs=in_specs, out_specs=out_specs, check_vma=False
    )
```

profile of v0, /device:TPU:0, one launch (start us, length us, event | category | flops | bytes accessed | tf_op | source)
XLA Modules:
  0.0 34.0 jit_solution(11277301197418685896)
XLA Ops:
  0.0 0.0 copy-start.1
  0.0 0.8 %copy-done.1 = s32[64,128]{1,0:T(8,128)S(1)} copy-done((s32[64,128]{1,0:T(8,128)S(1)}, s32[64,128]{1,0:T(8,128)}, u32[]{:S(2)}) %copy-start.1) | copy-done | bytes 32792
  0.8 0.0 copy-start.2
  0.8 3.0 %pack.1 = (f32[5,64,128]{2,1,0:T(8,128)S(1)}, f32[5,64,128]{2,1,0:T(8,128)S(1)}, f32[64,128]{1,0:T(8,128)S(1)}, f32[4,64,128]{2,1,0:T(8,128)S(1)}, f32[4,64,128]...) custom-call(f32[2,20,64,128]{3,2,1,0:T(8,128)} %t_hbm.1, ...), custom_call_target="tpu_custom_call" | custom-call | flops 1000000 | bytes 3932160 | tf_op jit(solution)/shard_map/pack/pallas_call | solution.py:55
  3.8 3.4 %collective-permute-start = (f32[4,64,128]{2,1,0:T(8,128)S(1)}, f32[4,64,128]{2,1,0:T(8,128)S(1)}, u32[]{:S(2)}, u32[]{:S(2)}) collective-permute-start(f32[4,64,128]{2,1,0:T(8,128)S(1)} %get-tuple-element.53), channel_id=1, source_target_pairs={{4,0},{8,4},{12,8},{16,12},{20,16},{24,20},{28,24},{0,28},{5,1},{9... | collective-permute-start | bytes 393224 | tf_op jit(solution)/shard_map/lon_halo/ppermute | solution.py:839
  7.2 0.0 collective-permute-start.1
  7.2 0.0 copy-done.2
  7.2 0.4 %factor.1 = (f32[20,64,128]{2,1,0:T(8,128)S(1)}, f32[20,64,128]{2,1,0:T(8,128)S(1)}, f32[20,64,128]{2,1,0:T(8,128)S(1)}, f32[20,64,128]{2,1,0:T(8,128)S(1)}, f32...) custom-call(f32[20,64,128]{2,1,0:T(8,128)S(1)} %copy-done.2, ...), custom_call_target="tpu_custom_call" | custom-call | flops 10000000 | bytes 3932160 | tf_op jit(solution)/shard_map/factor/pallas_call | solution.py:55
  7.6 1.6 %collective-permute-start.2 = (f32[3,64,128]{2,1,0:T(8,128)S(1)}, f32[3,64,128]{2,1,0:T(8,128)S(1)}, u32[]{:S(2)}, u32[]{:S(2)}) collective-permute-start(f32[3,64,128]{2,1,0:T(8,128)S(1)} %get-tuple-element.55), channel_id=1, source_target_pairs={{0,1},{1,0},{2,3},{3,2},{4,5},{5,4},{6,7},{7,6},{8,9},{9,8},{10,11... | collective-permute-start | bytes 294920 | tf_op jit(solution)/shard_map/pair_coefficients/ppermute | solution.py:848
  9.2 0.3 own_strips.1
  9.5 1.7 %advect_south.1.south_half = f32[2,10,64,128]{3,2,1,0:T(8,128)S(1)} custom-call(f32[20,64,128]{2,1,0:T(8,128)S(1)} %get-tuple-element.42.t0_ref, f32[20,64,128]{2,1,0:T(8,128)S(1)} %get-tuple-element.43.t1_ref, f32[20,64,128]{2,1,0:T(8,128)S(1)} %get-tuple-element.44.u_ref, f32[20,64,128]{2,1,0:T(8,128)S(1)} %get-tuple-element.45.v_ref, ...), custom_call_target="tpu_custom_call" | custom-call | flops 10000000 | bytes 2621440 | tf_op jit(solution)/shard_map/advect_south/pallas_call | solution.py:55
  11.2 0.0 copy-start
  11.2 1.7 %advect_north.1.north_half = f32[2,10,64,128]{3,2,1,0:T(8,128)S(1)} custom-call(f32[20,64,128]{2,1,0:T(8,128)S(1)} %get-tuple-element.42.t0_ref, f32[20,64,128]{2,1,0:T(8,128)S(1)} %get-tuple-element.43.t1_ref, f32[20,64,128]{2,1,0:T(8,128)S(1)} %get-tuple-element.44.u_ref, f32[20,64,128]{2,1,0:T(8,128)S(1)} %get-tuple-element.45.v_ref, ...), custom_call_target="tpu_custom_call" | custom-call | flops 10000000 | bytes 2621440 | tf_op jit(solution)/shard_map/advect_north/pallas_call | solution.py:55
  12.9 0.0 collective-permute-done.2.pair_ref
  12.9 0.0 collective-permute-done.re_ref
  12.9 0.0 collective-permute-done.1.rw_ref
  13.0 0.0 copy-done
  13.0 1.6 %advect_edge.1 = (f32[2,5,64,128]{3,2,1,0:T(8,128)S(1)}, f32[5,64,128]{2,1,0:T(8,128)S(1)}, f32[64,128]{1,0:T(8,128)S(1)}, f32[64,128]{1,0:T(8,128)S(1)}, f32[27...) custom-call(f32[4,5,64,128]{3,2,1,0:T(8,128)S(1)} %get-tuple-element.51.own_ref, ...), custom_call_target="tpu_custom_call" | custom-call | flops 1000000 | bytes 1966080 | tf_op jit(solution)/shard_map/advect_edge/pallas_call | solution.py:55
  14.6 0.1 collective-permute-start.4
  14.7 3.1 %collective-permute-start.3 = (f32[272,128]{1,0:T(8,128)S(1)}, f32[272,128]{1,0:T(8,128)S(1)}, u32[]{:S(2)}, u32[]{:S(2)}) collective-permute-start(f32[272,128]{1,0:T(8,128)S(1)} %get-tuple-element.65), channel_id=1, source_target_pairs={{0,1},{1,0},{2,3},{3,2},{4,5},{5,4},{6,7},{7,6},{8,9},{9,8},{10,11... | collective-permute-start | bytes 417800 | tf_op jit(solution)/shard_map/dep_halo/ppermute | solution.py:890
  17.8 2.4 %patch.1 = (f32[2,20,64,128]{3,2,1,0:T(8,128)S(1)}, f32[2,20,64,128]{3,2,1,0:T(8,128)S(1)}, f32[2,5,64,128]{3,2,1,0:T(8,128)S(1)}) custom-call(f32[2,10,64,128]{3,2,1,0:T(8,128)S(1)} %advect_north.1.north_half, f32[2,10,64,128]{3,2,1,0:T(8,128)S(1)} %advect_south.1.south_half, f32[2,5,64,128]{3,2,1,0:T(8,128)S(1)} %get-tuple-element.56.ea_ref, ...), custom_call_target="tpu_custom_call" | custom-call | flops 10000000 | bytes 5242880 | tf_op jit(solution)/shard_map/patch/pallas_call | solution.py:55
  20.2 2.5 %fluxes.1 = (f32[2,20,64,128]{3,2,1,0:T(8,128)S(1)}, f32[2,20,64,128]{3,2,1,0:T(8,128)S(1)}) custom-call(f32[2,20,64,128]{3,2,1,0:T(8,128)S(1)} %get-tuple-element.59.full_ref, f32[2,20,64,128]{3,2,1,0:T(8,128)S(1)} %get-tuple-element.60.gx_ref, f32[2,5,64,128]{3,2,1,0:T(8,128)S(1)} %get-tuple-element.61.efx_ref, f32[64,128]{1,0:T(8,128)S(1)} %get-tuple-element.62.bmx_ref, ...), custom_call_target="tpu_custom_call" | custom-call | flops 10000000 | bytes 6553600 | tf_op jit(solution)/shard_map/fluxes/pallas_call | solution.py:55
  22.8 0.0 collective-permute-done.3.first_ref
  22.8 0.0 collective-permute-done.4.second_ref
  22.8 1.4 %solve.1 = (f32[2,20,64,128]{3,2,1,0:T(8,128)S(1)}, f32[2,64,128]{2,1,0:T(8,128)S(1)}, f32[2,64,128]{2,1,0:T(8,128)S(1)}, f32[2,64,128]{2,1,0:T(8,128)S(1)}, f32...) custom-call(f32[2,20,64,128]{3,2,1,0:T(8,128)S(1)} %get-tuple-element.59.full_ref, ...), custom_call_target="tpu_custom_call" | custom-call | flops 10000000 | bytes 7864320 | tf_op jit(solution)/shard_map/solve/pallas_call | solution.py:55
  24.2 1.1 %collective-permute-start.5 = (f32[2,64,128]{2,1,0:T(8,128)S(1)}, f32[2,64,128]{2,1,0:T(8,128)S(1)}, u32[]{:S(2)}, u32[]{:S(2)}) collective-permute-start(f32[2,64,128]{2,1,0:T(8,128)S(1)} %get-tuple-element.75), channel_id=1, source_target_pairs={{0,3},{1,2},{2,1},{3,0},{4,7},{5,6},{6,5},{7,4},{8,11},{9,10},{10,... | collective-permute-start | bytes 196616 | tf_op jit(solution)/shard_map/interfaces/ppermute | solution.py:917
  25.3 0.5 %collective-permute-start.6 = (f32[2,64,128]{2,1,0:T(8,128)S(1)}, f32[2,64,128]{2,1,0:T(8,128)S(1)}, u32[]{:S(2)}, u32[]{:S(2)}) collective-permute-start(f32[2,64,128]{2,1,0:T(8,128)S(1)} %get-tuple-element.76), channel_id=1, source_target_pairs={{0,2},{1,3},{2,0},{3,1},{4,6},{5,7},{6,4},{7,5},{8,10},{9,11},{10,... | collective-permute-start | bytes 196616 | tf_op jit(solution)/shard_map/interfaces/ppermute | solution.py:918
  25.8 2.8 %collective-permute-start.7 = (f32[2,64,128]{2,1,0:T(8,128)S(1)}, f32[2,64,128]{2,1,0:T(8,128)S(1)}, u32[]{:S(2)}, u32[]{:S(2)}) collective-permute-start(f32[2,64,128]{2,1,0:T(8,128)S(1)} %get-tuple-element.77), channel_id=1, source_target_pairs={{0,1},{1,0},{2,3},{3,2},{4,5},{5,4},{6,7},{7,6},{8,9},{9,8},{10,11... | collective-permute-start | bytes 196616 | tf_op jit(solution)/shard_map/interfaces/ppermute | solution.py:919
  28.6 0.0 collective-permute-start.8
  28.6 4.0 %collective-permute-done.8.both_ref = f32[64,128]{1,0:T(8,128)S(1)} collective-permute-done((f32[64,128]{1,0:T(8,128)S(1)}, f32[64,128]{1,0:T(8,128)S(1)}, u32[]{:S(2)}, u32[]{:S(2)}) %collective-permute-start.8) | collective-permute-done | bytes 32800 | tf_op jit(solution)/shard_map/interfaces/ppermute | solution.py:920
  32.7 0.0 collective-permute-done.5.r3_ref
  32.7 0.0 collective-permute-done.6.r2_ref
  32.7 0.0 collective-permute-done.7.r1_ref
  32.7 1.2 %finish.1 = f32[2,20,64,128]{3,2,1,0:T(8,128)} custom-call(f32[2,20,64,128]{3,2,1,0:T(8,128)S(1)} %get-tuple-element.71.y_ref, f32[20,64,128]{2,1,0:T(8,128)S(1)} %get-tuple-element.72.a_ref, f32[20,64,128]{2,1,0:T(8,128)S(1)} %get-tuple-element.73.bb_ref, f32[3,64,128]{2,1,0:T(8,128)S(1)} %get-tuple-element.74.own_ref, ...), custom_call_target="tpu_custom_call" | custom-call | flops 1000000 | bytes 3932160 | tf_op jit(solution)/shard_map/finish/pallas_call | solution.py:55
Async XLA Ops:
  0.0 0.8 %copy-start.1 = (s32[64,128]{1,0:T(8,128)S(1)}, s32[64,128]{1,0:T(8,128)}, u32[]{:S(2)}) copy-start(s32[64,128]{1,0:T(8,128)} %b_ref.11) | copy-start | bytes 98308
  0.8 6.4 %copy-start.2 = (f32[20,64,128]{2,1,0:T(8,128)S(1)}, f32[20,64,128]{2,1,0:T(8,128)}, u32[]{:S(2)}) copy-start(f32[20,64,128]{2,1,0:T(8,128)} %kv_ref.1) | copy-start | bytes 1966084
  3.8 9.2 %collective-permute-start = (f32[4,64,128]{2,1,0:T(8,128)S(1)}, f32[4,64,128]{2,1,0:T(8,128)S(1)}, u32[]{:S(2)}, u32[]{:S(2)}) collective-permute-start(f32[4,64,128]{2,1,0:T(8,128)S(1)} %get-tuple-element.53), channel_id=1, source_target_pairs={{4,0},{8,4},{12,8},{16,12},{20,16},{24,20},{28,24},{0,28},{5,1},{9... | collective-permute-start | bytes 393224 | tf_op jit(solution)/shard_map/lon_halo/ppermute | solution.py:839
  7.2 5.8 %collective-permute-start.1 = (f32[4,64,128]{2,1,0:T(8,128)S(1)}, f32[4,64,128]{2,1,0:T(8,128)S(1)}, u32[]{:S(2)}, u32[]{:S(2)}) collective-permute-start(f32[4,64,128]{2,1,0:T(8,128)S(1)} %get-tuple-element.54), channel_id=1, source_target_pairs={{0,4},{4,8},{8,12},{12,16},{16,20},{20,24},{24,28},{28,0},{1,5},{5... | collective-permute-start | bytes 393224 | tf_op jit(solution)/shard_map/lon_halo/ppermute | solution.py:840
  7.6 5.4 %collective-permute-start.2 = (f32[3,64,128]{2,1,0:T(8,128)S(1)}, f32[3,64,128]{2,1,0:T(8,128)S(1)}, u32[]{:S(2)}, u32[]{:S(2)}) collective-permute-start(f32[3,64,128]{2,1,0:T(8,128)S(1)} %get-tuple-element.55), channel_id=1, source_target_pairs={{0,1},{1,0},{2,3},{3,2},{4,5},{5,4},{6,7},{7,6},{8,9},{9,8},{10,11... | collective-permute-start | bytes 294920 | tf_op jit(solution)/shard_map/pair_coefficients/ppermute | solution.py:848
  11.2 1.7 %copy-start = (f32[20,64,128]{2,1,0:T(8,128)S(1)}, f32[20,64,128]{2,1,0:T(8,128)}, u32[]{:S(2)}) copy-start(f32[20,64,128]{2,1,0:T(8,128)} %kh_ref.5) | copy-start | bytes 1966084
  14.6 8.2 %collective-permute-start.4 = (f32[400,128]{1,0:T(8,128)S(1)}, f32[400,128]{1,0:T(8,128)S(1)}, u32[]{:S(2)}, u32[]{:S(2)}) collective-permute-start(f32[400,128]{1,0:T(8,128)S(1)} %get-tuple-element.66), channel_id=1, source_target_pairs={{0,4},{1,2},{2,1},{3,7},{4,0},{5,6},{6,5},{7,3},{8,12},{9,10},{10,... | collective-permute-start | bytes 614408 | tf_op jit(solution)/shard_map/dep_halo/ppermute | solution.py:891
  14.7 8.1 %collective-permute-start.3 = (f32[272,128]{1,0:T(8,128)S(1)}, f32[272,128]{1,0:T(8,128)S(1)}, u32[]{:S(2)}, u32[]{:S(2)}) collective-permute-start(f32[272,128]{1,0:T(8,128)S(1)} %get-tuple-element.65), channel_id=1, source_target_pairs={{0,1},{1,0},{2,3},{3,2},{4,5},{5,4},{6,7},{7,6},{8,9},{9,8},{10,11... | collective-permute-start | bytes 417800 | tf_op jit(solution)/shard_map/dep_halo/ppermute | solution.py:890
  24.2 8.5 %collective-permute-start.5 = (f32[2,64,128]{2,1,0:T(8,128)S(1)}, f32[2,64,128]{2,1,0:T(8,128)S(1)}, u32[]{:S(2)}, u32[]{:S(2)}) collective-permute-start(f32[2,64,128]{2,1,0:T(8,128)S(1)} %get-tuple-element.75), channel_id=1, source_target_pairs={{0,3},{1,2},{2,1},{3,0},{4,7},{5,6},{6,5},{7,4},{8,11},{9,10},{10,... | collective-permute-start | bytes 196616 | tf_op jit(solution)/shard_map/interfaces/ppermute | solution.py:917
  25.3 7.4 %collective-permute-start.6 = (f32[2,64,128]{2,1,0:T(8,128)S(1)}, f32[2,64,128]{2,1,0:T(8,128)S(1)}, u32[]{:S(2)}, u32[]{:S(2)}) collective-permute-start(f32[2,64,128]{2,1,0:T(8,128)S(1)} %get-tuple-element.76), channel_id=1, source_target_pairs={{0,2},{1,3},{2,0},{3,1},{4,6},{5,7},{6,4},{7,5},{8,10},{9,11},{10,... | collective-permute-start | bytes 196616 | tf_op jit(solution)/shard_map/interfaces/ppermute | solution.py:918
  25.8 6.9 %collective-permute-start.7 = (f32[2,64,128]{2,1,0:T(8,128)S(1)}, f32[2,64,128]{2,1,0:T(8,128)S(1)}, u32[]{:S(2)}, u32[]{:S(2)}) collective-permute-start(f32[2,64,128]{2,1,0:T(8,128)S(1)} %get-tuple-element.77), channel_id=1, source_target_pairs={{0,1},{1,0},{2,3},{3,2},{4,5},{5,4},{6,7},{7,6},{8,9},{9,8},{10,11... | collective-permute-start | bytes 196616 | tf_op jit(solution)/shard_map/interfaces/ppermute | solution.py:919
  28.6 4.1 %collective-permute-start.8 = (f32[64,128]{1,0:T(8,128)S(1)}, f32[64,128]{1,0:T(8,128)S(1)}, u32[]{:S(2)}, u32[]{:S(2)}) collective-permute-start(f32[64,128]{1,0:T(8,128)S(1)} %get-tuple-element.78), channel_id=1, source_target_pairs={{0,1},{1,0},{2,3},{3,2},{4,5},{5,4},{6,7},{7,6},{8,9},{9,8},{10,11... | collective-permute-start | bytes 98312 | tf_op jit(solution)/shard_map/interfaces/ppermute | solution.py:920
where the time goes:
time: 34.1 us; the launch traced here: 34 us
  Pallas kernels  16.3 us (48%)
  starting transfers between devices  12.7 us (37%)
  waiting for transfers between devices  4.07 us (12%)
  local copies, waits for them, and re-layouts  0.77 us (2%)
    pallas_call x10, Pallas kernels, call(): pl.pallas_call(body, out_shape=out_shape, in_specs=in_specs or [VMEM] * l...  16.3 us
    ppermute x1, waiting for transfers between devices, per_device(): both = lax.ppermute(both, 'dep', swap)  4.05 us
    ppermute x1, starting transfers between devices, per_device(): r_east = lax.ppermute(ww, 'lon', west)  3.39 us
    ppermute x1, starting transfers between devices, per_device(): first = lax.ppermute(first, 'dep', swap)  3.14 us
    ppermute x1, starting transfers between devices, per_device(): m1 = lax.ppermute(m1, 'dep', swap)  2.83 us
    ppermute x1, starting transfers between devices, per_device(): pair = lax.ppermute(msg, 'dep', swap)  1.64 us
    ppermute x1, starting transfers between devices, per_device(): m3 = lax.ppermute(m3, 'dep', [(i, i ^ 3) for i in range(dep_n)])  1.14 us
    unnamed x6, local copies, waits for them, and re-layouts  0.77 us
  transfers between devices with their start and end apart: 9, of which 1 were waited for; matrix products, arithmetic and copies ran while one was open for 0% of the time, Pallas kernels for 26%

commit v1 on v0

--- a/solution.py
+++ b/solution.py
@@ -70,7 +70,7 @@
 def pack_kernel(
     t_hbm, u_hbm, v_hbm, kh_hbm, b_hbm,
     sw_ref, se_ref, bp_ref, ww_ref, we_ref, t0_ref, t1_ref, u_ref, v_ref, khb_ref,
-    kh_buf, b_buf, first_buf, sems, more_sems,
+    kh_buf, b_buf, first_buf, kappa_buf, sems, more_sems,
 ):
     rows_e = u_ref.shape[0] // GROUPS
     lat = u_ref.shape[1]
@@ -89,9 +89,35 @@
         pltpu.make_async_copy(b_hbm, b_buf, more_sems.at[0]),
         pltpu.make_async_copy(kh_hbm, kh_buf, more_sems.at[1]),
     ]
-    for copy in sum(groups, []) + tail:
+    half = GROUPS // 2
+    for copy in sum(groups[:half], []) + tail + sum(groups[half:], []):
         copy.start()
+    def arrange():
+        for copy in tail:
+            copy.wait()
+        bottom = slab_of(b_buf).astype(jnp.float32)
+        place = bottom
+        for g in range(1, GROUPS):
+            place = jnp.where(lane >= STRIP * g - 8, roll_lanes(bottom, STRIP * g), place)
+        place = jnp.where(lane >= 120, bottom, place)
+        bp_ref[...] = place
+
+        def kappa(r):
+            out = None
+            for g in range(GROUPS):
+                rolled = roll_lanes(slab_of(kh_buf, g * rows_e + r), STRIP * g + 23)
+                out = rolled if g == 0 else jnp.where(lane >= STRIP * g + 8, rolled, out)
+            return out
+
+        arranged = [kappa(r) for r in range(rows_e)]
+        for r in range(rows_e):
+            kappa_buf[r] = arranged[r]
+        khb_ref[0] = slab_of(kh_buf, 0)
+        khb_ref[1] = slab_of(kh_buf, GROUPS * rows_e - 1)
+
     for g in range(GROUPS):
+        if g == GROUPS // 2:
+            arrange()
         for copy in groups[g]:
             copy.wait()
         for batch in (range(0, rows_e // 2), range(rows_e // 2, rows_e)):
@@ -122,31 +148,13 @@
                     first_buf[r] = rolled[r, 0]
                 sw_ref[r] = low
                 se_ref[r] = high
-    for copy in tail:
-        copy.wait()
-    bottom = slab_of(b_buf).astype(jnp.float32)
-    place = bottom
-    for g in range(1, GROUPS):
-        place = jnp.where(lane >= STRIP * g - 8, roll_lanes(bottom, STRIP * g), place)
-    place = jnp.where(lane >= 120, bottom, place)
-    bp_ref[...] = place
-
-    def kappa(r):
-        out = None
-        for g in range(GROUPS):
-            rolled = roll_lanes(slab_of(kh_buf, g * rows_e + r), STRIP * g + 23)
-            out = rolled if g == 0 else jnp.where(lane >= STRIP * g + 8, rolled, out)
-        return out
-
-    khb_ref[0] = slab_of(kh_buf, 0)
-    khb_ref[1] = slab_of(kh_buf, GROUPS * rows_e - 1)
     last = rows_e - 1
-    kappa_last = kappa(last)
+    kappa_last, place = kappa_buf[last], bp_ref[...]
     lane_q = lane % STRIP
     low_last, high_last = sw_ref[last], se_ref[last]
     wires = []
     for r in range(last):
-        k = kappa(r)
+        k = kappa_buf[r]
         low, high = sw_ref[r], se_ref[r]
         west = (low, roll_lanes(low, -2), roll_lanes(low, -4), roll_lanes(low, -6), k)
         east = (
@@ -829,7 +837,7 @@
             (slabs(rows_e),) * 2 + (slabs(),) + (slabs(rows_e - 1),) * 2 + (slabs(levels),) * 4
             + (slabs(2),),
             [
-                work(levels), pltpu.VMEM((lat, lon), jnp.int32), work(rows_e),
+                work(levels), pltpu.VMEM((lat, lon), jnp.int32), work(rows_e), work(rows_e),
                 pltpu.SemaphoreType.DMA((GROUPS, 4)), pltpu.SemaphoreType.DMA((2,)),
             ],
             (tracers, u_east, v_north, kappa_h, bottom), 10**6, 6 * levels * slab, 50.5,

time: 34.1 us -> 34.5 us (1.012)
  no operation moved by 1% of the time
where the time goes in v1:
time: 34.5 us; the launch traced here: 34.3 us
  Pallas kernels  16.6 us (48%)
  starting transfers between devices  12.7 us (37%)
  waiting for transfers between devices  4.07 us (12%)
  local copies, waits for them, and re-layouts  0.77 us (2%)
    pallas_call x10, Pallas kernels, call(): pl.pallas_call(body, out_shape=out_shape, in_specs=in_specs or [VMEM] * l...  16.6 us
    ppermute x1, waiting for transfers between devices, per_device(): both = lax.ppermute(both, 'dep', swap)  4.05 us
    ppermute x1, starting transfers between devices, per_device(): r_east = lax.ppermute(ww, 'lon', west)  3.39 us
    ppermute x1, starting transfers between devices, per_device(): first = lax.ppermute(first, 'dep', swap)  3.14 us
    ppermute x1, starting transfers between devices, per_device(): m1 = lax.ppermute(m1, 'dep', swap)  2.83 us
    ppermute x1, starting transfers between devices, per_device(): pair = lax.ppermute(msg, 'dep', swap)  1.64 us
    ppermute x1, starting transfers between devices, per_device(): m3 = lax.ppermute(m3, 'dep', [(i, i ^ 3) for i in range(dep_n)])  1.14 us
    unnamed x6, local copies, waits for them, and re-layouts  0.77 us
  transfers between devices with their start and end apart: 9, of which 1 were waited for; matrix products, arithmetic and copies ran while one was open for 0% of the time, Pallas kernels for 26%

profile of v1, /device:TPU:0, one launch (start us, length us, event | category | flops | bytes accessed | tf_op | source)
XLA Modules:
  0.0 34.3 jit_solution(4571165760483368844)
XLA Ops:
  0.0 0.0 copy-start.1
  0.0 0.8 %copy-done.1 = s32[64,128]{1,0:T(8,128)S(1)} copy-done((s32[64,128]{1,0:T(8,128)S(1)}, s32[64,128]{1,0:T(8,128)}, u32[]{:S(2)}) %copy-start.1) | copy-done | bytes 32792
  0.8 0.0 copy-start.2
  0.8 3.3 %pack.1 = (f32[5,64,128]{2,1,0:T(8,128)S(1)}, f32[5,64,128]{2,1,0:T(8,128)S(1)}, f32[64,128]{1,0:T(8,128)S(1)}, f32[4,64,128]{2,1,0:T(8,128)S(1)}, f32[4,64,128]...) custom-call(f32[2,20,64,128]{3,2,1,0:T(8,128)} %t_hbm.1, ...), custom_call_target="tpu_custom_call" | custom-call | flops 1000000 | bytes 3932160 | tf_op jit(solution)/shard_map/pack/pallas_call | solution.py:55
  4.1 3.4 %collective-permute-start = (f32[4,64,128]{2,1,0:T(8,128)S(1)}, f32[4,64,128]{2,1,0:T(8,128)S(1)}, u32[]{:S(2)}, u32[]{:S(2)}) collective-permute-start(f32[4,64,128]{2,1,0:T(8,128)S(1)} %get-tuple-element.53), channel_id=1, source_target_pairs={{4,0},{8,4},{12,8},{16,12},{20,16},{24,20},{28,24},{0,28},{5,1},{9... | collective-permute-start | bytes 393224 | tf_op jit(solution)/shard_map/lon_halo/ppermute | solution.py:847
  7.5 0.0 collective-permute-start.1
  7.5 0.0 copy-done.2
  7.5 0.4 %factor.1 = (f32[20,64,128]{2,1,0:T(8,128)S(1)}, f32[20,64,128]{2,1,0:T(8,128)S(1)}, f32[20,64,128]{2,1,0:T(8,128)S(1)}, f32[20,64,128]{2,1,0:T(8,128)S(1)}, f32...) custom-call(f32[20,64,128]{2,1,0:T(8,128)S(1)} %copy-done.2, ...), custom_call_target="tpu_custom_call" | custom-call | flops 10000000 | bytes 3932160 | tf_op jit(solution)/shard_map/factor/pallas_call | solution.py:55
  7.9 1.6 %collective-permute-start.2 = (f32[3,64,128]{2,1,0:T(8,128)S(1)}, f32[3,64,128]{2,1,0:T(8,128)S(1)}, u32[]{:S(2)}, u32[]{:S(2)}) collective-permute-start(f32[3,64,128]{2,1,0:T(8,128)S(1)} %get-tuple-element.55), channel_id=1, source_target_pairs={{0,1},{1,0},{2,3},{3,2},{4,5},{5,4},{6,7},{7,6},{8,9},{9,8},{10,11... | collective-permute-start | bytes 294920 | tf_op jit(solution)/shard_map/pair_coefficients/ppermute | solution.py:856
  9.5 0.3 own_strips.1
  9.9 1.7 %advect_south.1.south_half = f32[2,10,64,128]{3,2,1,0:T(8,128)S(1)} custom-call(f32[20,64,128]{2,1,0:T(8,128)S(1)} %get-tuple-element.42.t0_ref, f32[20,64,128]{2,1,0:T(8,128)S(1)} %get-tuple-element.43.t1_ref, f32[20,64,128]{2,1,0:T(8,128)S(1)} %get-tuple-element.44.u_ref, f32[20,64,128]{2,1,0:T(8,128)S(1)} %get-tuple-element.45.v_ref, ...), custom_call_target="tpu_custom_call" | custom-call | flops 10000000 | bytes 2621440 | tf_op jit(solution)/shard_map/advect_south/pallas_call | solution.py:55
  11.6 0.0 copy-start
  11.6 1.7 %advect_north.1.north_half = f32[2,10,64,128]{3,2,1,0:T(8,128)S(1)} custom-call(f32[20,64,128]{2,1,0:T(8,128)S(1)} %get-tuple-element.42.t0_ref, f32[20,64,128]{2,1,0:T(8,128)S(1)} %get-tuple-element.43.t1_ref, f32[20,64,128]{2,1,0:T(8,128)S(1)} %get-tuple-element.44.u_ref, f32[20,64,128]{2,1,0:T(8,128)S(1)} %get-tuple-element.45.v_ref, ...), custom_call_target="tpu_custom_call" | custom-call | flops 10000000 | bytes 2621440 | tf_op jit(solution)/shard_map/advect_north/pallas_call | solution.py:55
  13.3 0.0 collective-permute-done.2.pair_ref
  13.3 0.0 collective-permute-done.re_ref
  13.3 0.0 collective-permute-done.1.rw_ref
  13.3 0.0 copy-done
  13.3 1.6 %advect_edge.1 = (f32[2,5,64,128]{3,2,1,0:T(8,128)S(1)}, f32[5,64,128]{2,1,0:T(8,128)S(1)}, f32[64,128]{1,0:T(8,128)S(1)}, f32[64,128]{1,0:T(8,128)S(1)}, f32[27...) custom-call(f32[4,5,64,128]{3,2,1,0:T(8,128)S(1)} %get-tuple-element.51.own_ref, ...), custom_call_target="tpu_custom_call" | custom-call | flops 1000000 | bytes 1966080 | tf_op jit(solution)/shard_map/advect_edge/pallas_call | solution.py:55
  14.9 0.1 collective-permute-start.4
  15.0 3.1 %collective-permute-start.3 = (f32[272,128]{1,0:T(8,128)S(1)}, f32[272,128]{1,0:T(8,128)S(1)}, u32[]{:S(2)}, u32[]{:S(2)}) collective-permute-start(f32[272,128]{1,0:T(8,128)S(1)} %get-tuple-element.65), channel_id=1, source_target_pairs={{0,1},{1,0},{2,3},{3,2},{4,5},{5,4},{6,7},{7,6},{8,9},{9,8},{10,11... | collective-permute-start | bytes 417800 | tf_op jit(solution)/shard_map/dep_halo/ppermute | solution.py:898
  18.1 2.4 %patch.1 = (f32[2,20,64,128]{3,2,1,0:T(8,128)S(1)}, f32[2,20,64,128]{3,2,1,0:T(8,128)S(1)}, f32[2,5,64,128]{3,2,1,0:T(8,128)S(1)}) custom-call(f32[2,10,64,128]{3,2,1,0:T(8,128)S(1)} %advect_north.1.north_half, f32[2,10,64,128]{3,2,1,0:T(8,128)S(1)} %advect_south.1.south_half, f32[2,5,64,128]{3,2,1,0:T(8,128)S(1)} %get-tuple-element.56.ea_ref, ...), custom_call_target="tpu_custom_call" | custom-call | flops 10000000 | bytes 5242880 | tf_op jit(solution)/shard_map/patch/pallas_call | solution.py:55
  20.5 2.5 %fluxes.1 = (f32[2,20,64,128]{3,2,1,0:T(8,128)S(1)}, f32[2,20,64,128]{3,2,1,0:T(8,128)S(1)}) custom-call(f32[2,20,64,128]{3,2,1,0:T(8,128)S(1)} %get-tuple-element.59.full_ref, f32[2,20,64,128]{3,2,1,0:T(8,128)S(1)} %get-tuple-element.60.gx_ref, f32[2,5,64,128]{3,2,1,0:T(8,128)S(1)} %get-tuple-element.61.efx_ref, f32[64,128]{1,0:T(8,128)S(1)} %get-tuple-element.62.bmx_ref, ...), custom_call_target="tpu_custom_call" | custom-call | flops 10000000 | bytes 6553600 | tf_op jit(solution)/shard_map/fluxes/pallas_call | solution.py:55
  23.1 0.0 collective-permute-done.3.first_ref
  23.1 0.0 collective-permute-done.4.second_ref
  23.1 1.4 %solve.1 = (f32[2,20,64,128]{3,2,1,0:T(8,128)S(1)}, f32[2,64,128]{2,1,0:T(8,128)S(1)}, f32[2,64,128]{2,1,0:T(8,128)S(1)}, f32[2,64,128]{2,1,0:T(8,128)S(1)}, f32...) custom-call(f32[2,20,64,128]{3,2,1,0:T(8,128)S(1)} %get-tuple-element.59.full_ref, ...), custom_call_target="tpu_custom_call" | custom-call | flops 10000000 | bytes 7864320 | tf_op jit(solution)/shard_map/solve/pallas_call | solution.py:55
  24.5 1.1 %collective-permute-start.5 = (f32[2,64,128]{2,1,0:T(8,128)S(1)}, f32[2,64,128]{2,1,0:T(8,128)S(1)}, u32[]{:S(2)}, u32[]{:S(2)}) collective-permute-start(f32[2,64,128]{2,1,0:T(8,128)S(1)} %get-tuple-element.75), channel_id=1, source_target_pairs={{0,3},{1,2},{2,1},{3,0},{4,7},{5,6},{6,5},{7,4},{8,11},{9,10},{10,... | collective-permute-start | bytes 196616 | tf_op jit(solution)/shard_map/interfaces/ppermute | solution.py:925
  25.6 0.5 %collective-permute-start.6 = (f32[2,64,128]{2,1,0:T(8,128)S(1)}, f32[2,64,128]{2,1,0:T(8,128)S(1)}, u32[]{:S(2)}, u32[]{:S(2)}) collective-permute-start(f32[2,64,128]{2,1,0:T(8,128)S(1)} %get-tuple-element.76), channel_id=1, source_target_pairs={{0,2},{1,3},{2,0},{3,1},{4,6},{5,7},{6,4},{7,5},{8,10},{9,11},{10,... | collective-permute-start | bytes 196616 | tf_op jit(solution)/shard_map/interfaces/ppermute | solution.py:926
  26.1 2.8 %collective-permute-start.7 = (f32[2,64,128]{2,1,0:T(8,128)S(1)}, f32[2,64,128]{2,1,0:T(8,128)S(1)}, u32[]{:S(2)}, u32[]{:S(2)}) collective-permute-start(f32[2,64,128]{2,1,0:T(8,128)S(1)} %get-tuple-element.77), channel_id=1, source_target_pairs={{0,1},{1,0},{2,3},{3,2},{4,5},{5,4},{6,7},{7,6},{8,9},{9,8},{10,11... | collective-permute-start | bytes 196616 | tf_op jit(solution)/shard_map/interfaces/ppermute | solution.py:927
  28.9 0.0 collective-permute-start.8
  29.0 4.0 %collective-permute-done.8.both_ref = f32[64,128]{1,0:T(8,128)S(1)} collective-permute-done((f32[64,128]{1,0:T(8,128)S(1)}, f32[64,128]{1,0:T(8,128)S(1)}, u32[]{:S(2)}, u32[]{:S(2)}) %collective-permute-start.8) | collective-permute-done | bytes 32800 | tf_op jit(solution)/shard_map/interfaces/ppermute | solution.py:928
  33.0 0.0 collective-permute-done.5.r3_ref
  33.0 0.0 collective-permute-done.6.r2_ref
  33.0 0.0 collective-permute-done.7.r1_ref
  33.0 1.2 %finish.1 = f32[2,20,64,128]{3,2,1,0:T(8,128)} custom-call(f32[2,20,64,128]{3,2,1,0:T(8,128)S(1)} %get-tuple-element.71.y_ref, f32[20,64,128]{2,1,0:T(8,128)S(1)} %get-tuple-element.72.a_ref, f32[20,64,128]{2,1,0:T(8,128)S(1)} %get-tuple-element.73.bb_ref, f32[3,64,128]{2,1,0:T(8,128)S(1)} %get-tuple-element.74.own_ref, ...), custom_call_target="tpu_custom_call" | custom-call | flops 1000000 | bytes 3932160 | tf_op jit(solution)/shard_map/finish/pallas_call | solution.py:55
Async XLA Ops:
  0.0 0.8 %copy-start.1 = (s32[64,128]{1,0:T(8,128)S(1)}, s32[64,128]{1,0:T(8,128)}, u32[]{:S(2)}) copy-start(s32[64,128]{1,0:T(8,128)} %b_ref.11) | copy-start | bytes 98308
  0.8 6.7 %copy-start.2 = (f32[20,64,128]{2,1,0:T(8,128)S(1)}, f32[20,64,128]{2,1,0:T(8,128)}, u32[]{:S(2)}) copy-start(f32[20,64,128]{2,1,0:T(8,128)} %kv_ref.1) | copy-start | bytes 1966084
  4.1 9.2 %collective-permute-start = (f32[4,64,128]{2,1,0:T(8,128)S(1)}, f32[4,64,128]{2,1,0:T(8,128)S(1)}, u32[]{:S(2)}, u32[]{:S(2)}) collective-permute-start(f32[4,64,128]{2,1,0:T(8,128)S(1)} %get-tuple-element.53), channel_id=1, source_target_pairs={{4,0},{8,4},{12,8},{16,12},{20,16},{24,20},{28,24},{0,28},{5,1},{9... | collective-permute-start | bytes 393224 | tf_op jit(solution)/shard_map/lon_halo/ppermute | solution.py:847
  7.5 5.8 %collective-permute-start.1 = (f32[4,64,128]{2,1,0:T(8,128)S(1)}, f32[4,64,128]{2,1,0:T(8,128)S(1)}, u32[]{:S(2)}, u32[]{:S(2)}) collective-permute-start(f32[4,64,128]{2,1,0:T(8,128)S(1)} %get-tuple-element.54), channel_id=1, source_target_pairs={{0,4},{4,8},{8,12},{12,16},{16,20},{20,24},{24,28},{28,0},{1,5},{5... | collective-permute-start | bytes 393224 | tf_op jit(solution)/shard_map/lon_halo/ppermute | solution.py:848
  7.9 5.4 %collective-permute-start.2 = (f32[3,64,128]{2,1,0:T(8,128)S(1)}, f32[3,64,128]{2,1,0:T(8,128)S(1)}, u32[]{:S(2)}, u32[]{:S(2)}) collective-permute-start(f32[3,64,128]{2,1,0:T(8,128)S(1)} %get-tuple-element.55), channel_id=1, source_target_pairs={{0,1},{1,0},{2,3},{3,2},{4,5},{5,4},{6,7},{7,6},{8,9},{9,8},{10,11... | collective-permute-start | bytes 294920 | tf_op jit(solution)/shard_map/pair_coefficients/ppermute | solution.py:856
  11.6 1.7 %copy-start = (f32[20,64,128]{2,1,0:T(8,128)S(1)}, f32[20,64,128]{2,1,0:T(8,128)}, u32[]{:S(2)}) copy-start(f32[20,64,128]{2,1,0:T(8,128)} %kh_ref.5) | copy-start | bytes 1966084
  14.9 8.2 %collective-permute-start.4 = (f32[400,128]{1,0:T(8,128)S(1)}, f32[400,128]{1,0:T(8,128)S(1)}, u32[]{:S(2)}, u32[]{:S(2)}) collective-permute-start(f32[400,128]{1,0:T(8,128)S(1)} %get-tuple-element.66), channel_id=1, source_target_pairs={{0,4},{1,2},{2,1},{3,7},{4,0},{5,6},{6,5},{7,3},{8,12},{9,10},{10,... | collective-permute-start | bytes 614408 | tf_op jit(solution)/shard_map/dep_halo/ppermute | solution.py:899
  15.0 8.1 %collective-permute-start.3 = (f32[272,128]{1,0:T(8,128)S(1)}, f32[272,128]{1,0:T(8,128)S(1)}, u32[]{:S(2)}, u32[]{:S(2)}) collective-permute-start(f32[272,128]{1,0:T(8,128)S(1)} %get-tuple-element.65), channel_id=1, source_target_pairs={{0,1},{1,0},{2,3},{3,2},{4,5},{5,4},{6,7},{7,6},{8,9},{9,8},{10,11... | collective-permute-start | bytes 417800 | tf_op jit(solution)/shard_map/dep_halo/ppermute | solution.py:898
  24.5 8.5 %collective-permute-start.5 = (f32[2,64,128]{2,1,0:T(8,128)S(1)}, f32[2,64,128]{2,1,0:T(8,128)S(1)}, u32[]{:S(2)}, u32[]{:S(2)}) collective-permute-start(f32[2,64,128]{2,1,0:T(8,128)S(1)} %get-tuple-element.75), channel_id=1, source_target_pairs={{0,3},{1,2},{2,1},{3,0},{4,7},{5,6},{6,5},{7,4},{8,11},{9,10},{10,... | collective-permute-start | bytes 196616 | tf_op jit(solution)/shard_map/interfaces/ppermute | solution.py:925
  25.6 7.4 %collective-permute-start.6 = (f32[2,64,128]{2,1,0:T(8,128)S(1)}, f32[2,64,128]{2,1,0:T(8,128)S(1)}, u32[]{:S(2)}, u32[]{:S(2)}) collective-permute-start(f32[2,64,128]{2,1,0:T(8,128)S(1)} %get-tuple-element.76), channel_id=1, source_target_pairs={{0,2},{1,3},{2,0},{3,1},{4,6},{5,7},{6,4},{7,5},{8,10},{9,11},{10,... | collective-permute-start | bytes 196616 | tf_op jit(solution)/shard_map/interfaces/ppermute | solution.py:926
  26.1 6.9 %collective-permute-start.7 = (f32[2,64,128]{2,1,0:T(8,128)S(1)}, f32[2,64,128]{2,1,0:T(8,128)S(1)}, u32[]{:S(2)}, u32[]{:S(2)}) collective-permute-start(f32[2,64,128]{2,1,0:T(8,128)S(1)} %get-tuple-element.77), channel_id=1, source_target_pairs={{0,1},{1,0},{2,3},{3,2},{4,5},{5,4},{6,7},{7,6},{8,9},{9,8},{10,11... | collective-permute-start | bytes 196616 | tf_op jit(solution)/shard_map/interfaces/ppermute | solution.py:927
  28.9 4.1 %collective-permute-start.8 = (f32[64,128]{1,0:T(8,128)S(1)}, f32[64,128]{1,0:T(8,128)S(1)}, u32[]{:S(2)}, u32[]{:S(2)}) collective-permute-start(f32[64,128]{1,0:T(8,128)S(1)} %get-tuple-element.78), channel_id=1, source_target_pairs={{0,1},{1,0},{2,3},{3,2},{4,5},{5,4},{6,7},{7,6},{8,9},{9,8},{10,11... | collective-permute-start | bytes 98312 | tf_op jit(solution)/shard_map/interfaces/ppermute | solution.py:928

commit v2 on v0

--- a/solution.py
+++ b/solution.py
@@ -649,7 +649,7 @@
 def solve_kernel(
     full_ref, q_ref, fz_ref, ea_ref, ek_ref, eb_ref, bmx_ref, b_ref, kh_ref,
     first_ref, second_ref, inv_ref, ei_ref, ratio_ref, red_ref, pair_ref,
-    y_ref, m3_ref, m2_ref, m1_ref, both_ref, own_ref,
+    y_ref, m2_ref, m3_ref, m1_ref, both_ref, own_ref,
     pad, epad, fze, halo,
 ):
     levels, lat = q_ref.shape[1], q_ref.shape[2]
@@ -768,7 +768,7 @@
 
 
 def finish_kernel(
-    y_ref, a_ref, bb_ref, own_ref, r3_ref, r2_ref, r1_ref, both_ref, out_hbm, out, sems
+    y_ref, a_ref, bb_ref, own_ref, r2_ref, r3_ref, r1_ref, both_ref, out_hbm, out, sems
 ):
     levels = y_ref.shape[1]
     me = lax.axis_index("dep")
@@ -901,7 +901,7 @@
             (full, gx, efx, bmx, bottom, kappa_h), 10**7, 10 * levels * slab, 16,
         )
     with jax.named_scope("solve"):
-        y, m3, m2, m1, both, own = call(
+        y, m2, m3, m1, both, own = call(
             solve_kernel, (slabs(2, levels), slabs(2), slabs(2), slabs(2), slabs(), slabs(3)),
             [
                 work(2, 10), work(2, rows_e + 2), work(2, 4),
@@ -914,15 +914,15 @@
             10**7, 12 * levels * slab, 24,
         )
     with jax.named_scope("interfaces"):
+        m2 = lax.ppermute(m2, "dep", [(i, i ^ 2) for i in range(dep_n)])
         m3 = lax.ppermute(m3, "dep", [(i, i ^ 3) for i in range(dep_n)])
-        m2 = lax.ppermute(m2, "dep", [(i, i ^ 2) for i in range(dep_n)])
         m1 = lax.ppermute(m1, "dep", swap)
         both = lax.ppermute(both, "dep", swap)
     with jax.named_scope("finish"):
         return call(
             finish_kernel, slabs(2, levels),
             [work(2, levels), pltpu.SemaphoreType.DMA((2, GROUPS))],
-            (y, a_end, b_end, own, m3, m2, m1, both), 10**6, 6 * levels * slab, 16,
+            (y, a_end, b_end, own, m2, m3, m1, both), 10**6, 6 * levels * slab, 16,
             out_specs=HBM,
         )
 

time: 34.1 us -> 33.8 us (level)
  waiting for transfers between devices: 4.07 us -> 3.67 us
    ppermute x1, starting transfers between devices: 2.83 us -> 1.03 us  [per_device(): m1 = lax.ppermute(m1, 'dep', swap)]
    ppermute x1, starting transfers between devices: 0.03 us -> 1 us  [per_device(): both = lax.ppermute(both, 'dep', swap)]
    ppermute x1, starting transfers between devices: 0.48 us -> 1.02 us  [per_device(): m2 = lax.ppermute(m2, 'dep', [(i, i ^ 2) for i in range(dep_n)])]
    ppermute x1, waiting for transfers between devices: 4.05 us -> 3.64 us  [per_device(): both = lax.ppermute(both, 'dep', swap)]
    ppermute x1, starting transfers between devices: 1.14 us -> 1.51 us  [per_device(): m3 = lax.ppermute(m3, 'dep', [(i, i ^ 3) for i in range(dep_n)])]
  transfers between devices with their start and end apart: 9 -> 9, of which waited for: 1 -> 1; matrix products, arithmetic and copies ran while one was open for 0% -> 0% of each run, Pallas kernels for 26% -> 27%
where the time goes in v2:
time: 33.8 us; the launch traced here: 33.6 us
  Pallas kernels  16.3 us (48%)
  starting transfers between devices  12.8 us (38%)
  waiting for transfers between devices  3.67 us (11%)
  local copies, waits for them, and re-layouts  0.77 us (2%)
    pallas_call x10, Pallas kernels, call(): pl.pallas_call(body, out_shape=out_shape, in_specs=in_specs or [VMEM] * l...  16.3 us
    ppermute x1, waiting for transfers between devices, per_device(): both = lax.ppermute(both, 'dep', swap)  3.64 us
    ppermute x1, starting transfers between devices, per_device(): r_east = lax.ppermute(ww, 'lon', west)  3.39 us
    ppermute x1, starting transfers between devices, per_device(): first = lax.ppermute(first, 'dep', swap)  3.14 us
    ppermute x1, starting transfers between devices, per_device(): pair = lax.ppermute(msg, 'dep', swap)  1.64 us
    ppermute x1, starting transfers between devices, per_device(): m3 = lax.ppermute(m3, 'dep', [(i, i ^ 3) for i in range(dep_n)])  1.51 us
    ppermute x1, starting transfers between devices, per_device(): m1 = lax.ppermute(m1, 'dep', swap)  1.03 us
    ppermute x1, starting transfers between devices, per_device(): m2 = lax.ppermute(m2, 'dep', [(i, i ^ 2) for i in range(dep_n)])  1.02 us
  transfers between devices with their start and end apart: 9, of which 1 were waited for; matrix products, arithmetic and copies ran while one was open for 0% of the time, Pallas kernels for 27%

profile of v2, /device:TPU:0, one launch (start us, length us, event | category | flops | bytes accessed | tf_op | source)
XLA Modules:
  0.0 33.6 jit_solution(9834958147028231531)
XLA Ops:
  0.0 0.0 copy-start.1
  0.0 0.8 %copy-done.1 = s32[64,128]{1,0:T(8,128)S(1)} copy-done((s32[64,128]{1,0:T(8,128)S(1)}, s32[64,128]{1,0:T(8,128)}, u32[]{:S(2)}) %copy-start.1) | copy-done | bytes 32792
  0.8 0.0 copy-start.2
  0.8 3.0 %pack.1 = (f32[5,64,128]{2,1,0:T(8,128)S(1)}, f32[5,64,128]{2,1,0:T(8,128)S(1)}, f32[64,128]{1,0:T(8,128)S(1)}, f32[4,64,128]{2,1,0:T(8,128)S(1)}, f32[4,64,128]...) custom-call(f32[2,20,64,128]{3,2,1,0:T(8,128)} %t_hbm.1, ...), custom_call_target="tpu_custom_call" | custom-call | flops 1000000 | bytes 3932160 | tf_op jit(solution)/shard_map/pack/pallas_call | solution.py:55
  3.8 3.4 %collective-permute-start = (f32[4,64,128]{2,1,0:T(8,128)S(1)}, f32[4,64,128]{2,1,0:T(8,128)S(1)}, u32[]{:S(2)}, u32[]{:S(2)}) collective-permute-start(f32[4,64,128]{2,1,0:T(8,128)S(1)} %get-tuple-element.53), channel_id=1, source_target_pairs={{4,0},{8,4},{12,8},{16,12},{20,16},{24,20},{28,24},{0,28},{5,1},{9... | collective-permute-start | bytes 393224 | tf_op jit(solution)/shard_map/lon_halo/ppermute | solution.py:839
  7.2 0.0 collective-permute-start.1
  7.2 0.0 copy-done.2
  7.2 0.4 %factor.1 = (f32[20,64,128]{2,1,0:T(8,128)S(1)}, f32[20,64,128]{2,1,0:T(8,128)S(1)}, f32[20,64,128]{2,1,0:T(8,128)S(1)}, f32[20,64,128]{2,1,0:T(8,128)S(1)}, f32...) custom-call(f32[20,64,128]{2,1,0:T(8,128)S(1)} %copy-done.2, ...), custom_call_target="tpu_custom_call" | custom-call | flops 10000000 | bytes 3932160 | tf_op jit(solution)/shard_map/factor/pallas_call | solution.py:55
  7.6 1.6 %collective-permute-start.2 = (f32[3,64,128]{2,1,0:T(8,128)S(1)}, f32[3,64,128]{2,1,0:T(8,128)S(1)}, u32[]{:S(2)}, u32[]{:S(2)}) collective-permute-start(f32[3,64,128]{2,1,0:T(8,128)S(1)} %get-tuple-element.55), channel_id=1, source_target_pairs={{0,1},{1,0},{2,3},{3,2},{4,5},{5,4},{6,7},{7,6},{8,9},{9,8},{10,11... | collective-permute-start | bytes 294920 | tf_op jit(solution)/shard_map/pair_coefficients/ppermute | solution.py:848
  9.2 0.3 own_strips.1
  9.5 1.7 %advect_south.1.south_half = f32[2,10,64,128]{3,2,1,0:T(8,128)S(1)} custom-call(f32[20,64,128]{2,1,0:T(8,128)S(1)} %get-tuple-element.42.t0_ref, f32[20,64,128]{2,1,0:T(8,128)S(1)} %get-tuple-element.43.t1_ref, f32[20,64,128]{2,1,0:T(8,128)S(1)} %get-tuple-element.44.u_ref, f32[20,64,128]{2,1,0:T(8,128)S(1)} %get-tuple-element.45.v_ref, ...), custom_call_target="tpu_custom_call" | custom-call | flops 10000000 | bytes 2621440 | tf_op jit(solution)/shard_map/advect_south/pallas_call | solution.py:55
  11.2 0.0 copy-start
  11.2 1.7 %advect_north.1.north_half = f32[2,10,64,128]{3,2,1,0:T(8,128)S(1)} custom-call(f32[20,64,128]{2,1,0:T(8,128)S(1)} %get-tuple-element.42.t0_ref, f32[20,64,128]{2,1,0:T(8,128)S(1)} %get-tuple-element.43.t1_ref, f32[20,64,128]{2,1,0:T(8,128)S(1)} %get-tuple-element.44.u_ref, f32[20,64,128]{2,1,0:T(8,128)S(1)} %get-tuple-element.45.v_ref, ...), custom_call_target="tpu_custom_call" | custom-call | flops 10000000 | bytes 2621440 | tf_op jit(solution)/shard_map/advect_north/pallas_call | solution.py:55
  12.9 0.0 collective-permute-done.2.pair_ref
  12.9 0.0 collective-permute-done.re_ref
  12.9 0.0 collective-permute-done.1.rw_ref
  13.0 0.0 copy-done
  13.0 1.6 %advect_edge.1 = (f32[2,5,64,128]{3,2,1,0:T(8,128)S(1)}, f32[5,64,128]{2,1,0:T(8,128)S(1)}, f32[64,128]{1,0:T(8,128)S(1)}, f32[64,128]{1,0:T(8,128)S(1)}, f32[27...) custom-call(f32[4,5,64,128]{3,2,1,0:T(8,128)S(1)} %get-tuple-element.51.own_ref, ...), custom_call_target="tpu_custom_call" | custom-call | flops 1000000 | bytes 1966080 | tf_op jit(solution)/shard_map/advect_edge/pallas_call | solution.py:55
  14.6 0.1 collective-permute-start.4
  14.7 3.1 %collective-permute-start.3 = (f32[272,128]{1,0:T(8,128)S(1)}, f32[272,128]{1,0:T(8,128)S(1)}, u32[]{:S(2)}, u32[]{:S(2)}) collective-permute-start(f32[272,128]{1,0:T(8,128)S(1)} %get-tuple-element.65), channel_id=1, source_target_pairs={{0,1},{1,0},{2,3},{3,2},{4,5},{5,4},{6,7},{7,6},{8,9},{9,8},{10,11... | collective-permute-start | bytes 417800 | tf_op jit(solution)/shard_map/dep_halo/ppermute | solution.py:890
  17.8 2.4 %patch.1 = (f32[2,20,64,128]{3,2,1,0:T(8,128)S(1)}, f32[2,20,64,128]{3,2,1,0:T(8,128)S(1)}, f32[2,5,64,128]{3,2,1,0:T(8,128)S(1)}) custom-call(f32[2,10,64,128]{3,2,1,0:T(8,128)S(1)} %advect_north.1.north_half, f32[2,10,64,128]{3,2,1,0:T(8,128)S(1)} %advect_south.1.south_half, f32[2,5,64,128]{3,2,1,0:T(8,128)S(1)} %get-tuple-element.56.ea_ref, ...), custom_call_target="tpu_custom_call" | custom-call | flops 10000000 | bytes 5242880 | tf_op jit(solution)/shard_map/patch/pallas_call | solution.py:55
  20.2 2.5 %fluxes.1 = (f32[2,20,64,128]{3,2,1,0:T(8,128)S(1)}, f32[2,20,64,128]{3,2,1,0:T(8,128)S(1)}) custom-call(f32[2,20,64,128]{3,2,1,0:T(8,128)S(1)} %get-tuple-element.59.full_ref, f32[2,20,64,128]{3,2,1,0:T(8,128)S(1)} %get-tuple-element.60.gx_ref, f32[2,5,64,128]{3,2,1,0:T(8,128)S(1)} %get-tuple-element.61.efx_ref, f32[64,128]{1,0:T(8,128)S(1)} %get-tuple-element.62.bmx_ref, ...), custom_call_target="tpu_custom_call" | custom-call | flops 10000000 | bytes 6553600 | tf_op jit(solution)/shard_map/fluxes/pallas_call | solution.py:55
  22.8 0.0 collective-permute-done.3.first_ref
  22.8 0.0 collective-permute-done.4.second_ref
  22.8 1.4 %solve.1 = (f32[2,20,64,128]{3,2,1,0:T(8,128)S(1)}, f32[2,64,128]{2,1,0:T(8,128)S(1)}, f32[2,64,128]{2,1,0:T(8,128)S(1)}, f32[2,64,128]{2,1,0:T(8,128)S(1)}, f32...) custom-call(f32[2,20,64,128]{3,2,1,0:T(8,128)S(1)} %get-tuple-element.59.full_ref, ...), custom_call_target="tpu_custom_call" | custom-call | flops 10000000 | bytes 7864320 | tf_op jit(solution)/shard_map/solve/pallas_call | solution.py:55
  24.2 1.0 %collective-permute-start.5 = (f32[2,64,128]{2,1,0:T(8,128)S(1)}, f32[2,64,128]{2,1,0:T(8,128)S(1)}, u32[]{:S(2)}, u32[]{:S(2)}) collective-permute-start(f32[2,64,128]{2,1,0:T(8,128)S(1)} %get-tuple-element.75), channel_id=1, source_target_pairs={{0,2},{1,3},{2,0},{3,1},{4,6},{5,7},{6,4},{7,5},{8,10},{9,11},{10,... | collective-permute-start | bytes 196616 | tf_op jit(solution)/shard_map/interfaces/ppermute | solution.py:917
  25.2 1.5 %collective-permute-start.6 = (f32[2,64,128]{2,1,0:T(8,128)S(1)}, f32[2,64,128]{2,1,0:T(8,128)S(1)}, u32[]{:S(2)}, u32[]{:S(2)}) collective-permute-start(f32[2,64,128]{2,1,0:T(8,128)S(1)} %get-tuple-element.76), channel_id=1, source_target_pairs={{0,3},{1,2},{2,1},{3,0},{4,7},{5,6},{6,5},{7,4},{8,11},{9,10},{10,... | collective-permute-start | bytes 196616 | tf_op jit(solution)/shard_map/interfaces/ppermute | solution.py:918
  26.7 1.0 %collective-permute-start.7 = (f32[2,64,128]{2,1,0:T(8,128)S(1)}, f32[2,64,128]{2,1,0:T(8,128)S(1)}, u32[]{:S(2)}, u32[]{:S(2)}) collective-permute-start(f32[2,64,128]{2,1,0:T(8,128)S(1)} %get-tuple-element.77), channel_id=1, source_target_pairs={{0,1},{1,0},{2,3},{3,2},{4,5},{5,4},{6,7},{7,6},{8,9},{9,8},{10,11... | collective-permute-start | bytes 196616 | tf_op jit(solution)/shard_map/interfaces/ppermute | solution.py:919
  27.7 1.0 %collective-permute-start.8 = (f32[64,128]{1,0:T(8,128)S(1)}, f32[64,128]{1,0:T(8,128)S(1)}, u32[]{:S(2)}, u32[]{:S(2)}) collective-permute-start(f32[64,128]{1,0:T(8,128)S(1)} %get-tuple-element.78), channel_id=1, source_target_pairs={{0,1},{1,0},{2,3},{3,2},{4,5},{5,4},{6,7},{7,6},{8,9},{9,8},{10,11... | collective-permute-start | bytes 98312 | tf_op jit(solution)/shard_map/interfaces/ppermute | solution.py:920
  28.7 3.6 %collective-permute-done.8.both_ref = f32[64,128]{1,0:T(8,128)S(1)} collective-permute-done((f32[64,128]{1,0:T(8,128)S(1)}, f32[64,128]{1,0:T(8,128)S(1)}, u32[]{:S(2)}, u32[]{:S(2)}) %collective-permute-start.8) | collective-permute-done | bytes 32800 | tf_op jit(solution)/shard_map/interfaces/ppermute | solution.py:920
  32.4 0.0 collective-permute-done.5.r2_ref
  32.4 0.0 collective-permute-done.6.r3_ref
  32.4 0.0 collective-permute-done.7.r1_ref
  32.4 1.2 %finish.1 = f32[2,20,64,128]{3,2,1,0:T(8,128)} custom-call(f32[2,20,64,128]{3,2,1,0:T(8,128)S(1)} %get-tuple-element.71.y_ref, f32[20,64,128]{2,1,0:T(8,128)S(1)} %get-tuple-element.72.a_ref, f32[20,64,128]{2,1,0:T(8,128)S(1)} %get-tuple-element.73.bb_ref, f32[3,64,128]{2,1,0:T(8,128)S(1)} %get-tuple-element.74.own_ref, ...), custom_call_target="tpu_custom_call" | custom-call | flops 1000000 | bytes 3932160 | tf_op jit(solution)/shard_map/finish/pallas_call | solution.py:55
Async XLA Ops:
  0.0 0.8 %copy-start.1 = (s32[64,128]{1,0:T(8,128)S(1)}, s32[64,128]{1,0:T(8,128)}, u32[]{:S(2)}) copy-start(s32[64,128]{1,0:T(8,128)} %b_ref.11) | copy-start | bytes 98308
  0.8 6.4 %copy-start.2 = (f32[20,64,128]{2,1,0:T(8,128)S(1)}, f32[20,64,128]{2,1,0:T(8,128)}, u32[]{:S(2)}) copy-start(f32[20,64,128]{2,1,0:T(8,128)} %kv_ref.1) | copy-start | bytes 1966084
  3.8 9.2 %collective-permute-start = (f32[4,64,128]{2,1,0:T(8,128)S(1)}, f32[4,64,128]{2,1,0:T(8,128)S(1)}, u32[]{:S(2)}, u32[]{:S(2)}) collective-permute-start(f32[4,64,128]{2,1,0:T(8,128)S(1)} %get-tuple-element.53), channel_id=1, source_target_pairs={{4,0},{8,4},{12,8},{16,12},{20,16},{24,20},{28,24},{0,28},{5,1},{9... | collective-permute-start | bytes 393224 | tf_op jit(solution)/shard_map/lon_halo/ppermute | solution.py:839
  7.2 5.8 %collective-permute-start.1 = (f32[4,64,128]{2,1,0:T(8,128)S(1)}, f32[4,64,128]{2,1,0:T(8,128)S(1)}, u32[]{:S(2)}, u32[]{:S(2)}) collective-permute-start(f32[4,64,128]{2,1,0:T(8,128)S(1)} %get-tuple-element.54), channel_id=1, source_target_pairs={{0,4},{4,8},{8,12},{12,16},{16,20},{20,24},{24,28},{28,0},{1,5},{5... | collective-permute-start | bytes 393224 | tf_op jit(solution)/shard_map/lon_halo/ppermute | solution.py:840
  7.6 5.4 %collective-permute-start.2 = (f32[3,64,128]{2,1,0:T(8,128)S(1)}, f32[3,64,128]{2,1,0:T(8,128)S(1)}, u32[]{:S(2)}, u32[]{:S(2)}) collective-permute-start(f32[3,64,128]{2,1,0:T(8,128)S(1)} %get-tuple-element.55), channel_id=1, source_target_pairs={{0,1},{1,0},{2,3},{3,2},{4,5},{5,4},{6,7},{7,6},{8,9},{9,8},{10,11... | collective-permute-start | bytes 294920 | tf_op jit(solution)/shard_map/pair_coefficients/ppermute | solution.py:848
  11.2 1.7 %copy-start = (f32[20,64,128]{2,1,0:T(8,128)S(1)}, f32[20,64,128]{2,1,0:T(8,128)}, u32[]{:S(2)}) copy-start(f32[20,64,128]{2,1,0:T(8,128)} %kh_ref.5) | copy-start | bytes 1966084
  14.6 8.2 %collective-permute-start.4 = (f32[400,128]{1,0:T(8,128)S(1)}, f32[400,128]{1,0:T(8,128)S(1)}, u32[]{:S(2)}, u32[]{:S(2)}) collective-permute-start(f32[400,128]{1,0:T(8,128)S(1)} %get-tuple-element.66), channel_id=1, source_target_pairs={{0,4},{1,2},{2,1},{3,7},{4,0},{5,6},{6,5},{7,3},{8,12},{9,10},{10,... | collective-permute-start | bytes 614408 | tf_op jit(solution)/shard_map/dep_halo/ppermute | solution.py:891
  14.7 8.1 %collective-permute-start.3 = (f32[272,128]{1,0:T(8,128)S(1)}, f32[272,128]{1,0:T(8,128)S(1)}, u32[]{:S(2)}, u32[]{:S(2)}) collective-permute-start(f32[272,128]{1,0:T(8,128)S(1)} %get-tuple-element.65), channel_id=1, source_target_pairs={{0,1},{1,0},{2,3},{3,2},{4,5},{5,4},{6,7},{7,6},{8,9},{9,8},{10,11... | collective-permute-start | bytes 417800 | tf_op jit(solution)/shard_map/dep_halo/ppermute | solution.py:890
  24.2 8.2 %collective-permute-start.5 = (f32[2,64,128]{2,1,0:T(8,128)S(1)}, f32[2,64,128]{2,1,0:T(8,128)S(1)}, u32[]{:S(2)}, u32[]{:S(2)}) collective-permute-start(f32[2,64,128]{2,1,0:T(8,128)S(1)} %get-tuple-element.75), channel_id=1, source_target_pairs={{0,2},{1,3},{2,0},{3,1},{4,6},{5,7},{6,4},{7,5},{8,10},{9,11},{10,... | collective-permute-start | bytes 196616 | tf_op jit(solution)/shard_map/interfaces/ppermute | solution.py:917
  25.2 7.2 %collective-permute-start.6 = (f32[2,64,128]{2,1,0:T(8,128)S(1)}, f32[2,64,128]{2,1,0:T(8,128)S(1)}, u32[]{:S(2)}, u32[]{:S(2)}) collective-permute-start(f32[2,64,128]{2,1,0:T(8,128)S(1)} %get-tuple-element.76), channel_id=1, source_target_pairs={{0,3},{1,2},{2,1},{3,0},{4,7},{5,6},{6,5},{7,4},{8,11},{9,10},{10,... | collective-permute-start | bytes 196616 | tf_op jit(solution)/shard_map/interfaces/ppermute | solution.py:918
  26.7 5.7 %collective-permute-start.7 = (f32[2,64,128]{2,1,0:T(8,128)S(1)}, f32[2,64,128]{2,1,0:T(8,128)S(1)}, u32[]{:S(2)}, u32[]{:S(2)}) collective-permute-start(f32[2,64,128]{2,1,0:T(8,128)S(1)} %get-tuple-element.77), channel_id=1, source_target_pairs={{0,1},{1,0},{2,3},{3,2},{4,5},{5,4},{6,7},{7,6},{8,9},{9,8},{10,11... | collective-permute-start | bytes 196616 | tf_op jit(solution)/shard_map/interfaces/ppermute | solution.py:919
  27.7 4.6 %collective-permute-start.8 = (f32[64,128]{1,0:T(8,128)S(1)}, f32[64,128]{1,0:T(8,128)S(1)}, u32[]{:S(2)}, u32[]{:S(2)}) collective-permute-start(f32[64,128]{1,0:T(8,128)S(1)} %get-tuple-element.78), channel_id=1, source_target_pairs={{0,1},{1,0},{2,3},{3,2},{4,5},{5,4},{6,7},{7,6},{8,9},{9,8},{10,11... | collective-permute-start | bytes 98312 | tf_op jit(solution)/shard_map/interfaces/ppermute | solution.py:920

commit v3 on v2

--- a/solution.py
+++ b/solution.py
@@ -150,19 +150,20 @@
         low, high = sw_ref[r], se_ref[r]
         west = (low, roll_lanes(low, -2), roll_lanes(low, -4), roll_lanes(low, -6), k)
         east = (
-            roll_lanes(high, 6), roll_lanes(high, 4), roll_lanes(high, 2), roll_lanes(high, -1),
-            roll_lanes(k, 1),
+            roll_lanes(high, -2), roll_lanes(high, -4), roll_lanes(high, -7), roll_lanes(k, -5),
         )
         west += (roll_lanes(low_last, 24 - 8 * r),)
-        east += (roll_lanes(high_last, 5 if r == 3 else 30 - 8 * r),)
+        east += (roll_lanes(high_last, -1 if r == 3 else 24 - 8 * r),)
         if r == 3:
             west += (roll_lanes(kappa_last, 6),)
-            east += (roll_lanes(kappa_last, 7),)
+            east += (roll_lanes(kappa_last, 1), high)
         else:
-            west += (roll_lanes(place, 30 - 2 * r),)
-            east += (roll_lanes(place, 36 - 2 * r),)
+            pair = roll_lanes(place, 30 - 2 * r)
+            west += (pair,)
+            east += (pair, high)
         starts = (6, 12, 18, 23, 24, 29 if r == 3 else 30)
-        for ref, parts in ((ww_ref, west), (we_ref, east)):
+        starts_e = (6, 12, 17, 18, 23 if r == 3 else 24, 26)
+        for ref, parts, starts in ((ww_ref, west, starts), (we_ref, east, starts_e)):
             wire = parts[0]
             for start, part in zip(starts, parts[1:]):
                 wire = jnp.where(lane_q >= start, part, wire)
@@ -328,7 +329,7 @@
     lane_q = lane % STRIP
     bottom = slab_of(b_ref).astype(jnp.float32)
     east = [roll_lanes(re_ref[r], 2 * r - 22) for r in range(3)]
-    west = [roll_lanes(rw_ref[r], 2 * r - 12) for r in range(3)]
+    west = [roll_lanes(rw_ref[r], 2 * r - 6) for r in range(3)]
     eb = join(
         lane_q,
         ownb_ref[...],
@@ -341,7 +342,7 @@
     bmx_ref[...] = jnp.minimum(b_west, b_east)
     last = rows_e - 1
     for r in range(rows_e):
-        at, shift_e, shift_w = (3, -21, -6) if r == last else (r, -15, 0)
+        at, shift_e, shift_w = (3, -21, 0) if r == last else (r, -15, 6)
         ek_ref[r] = jnp.where(
             lane_q < 16, roll_lanes(re_ref[at], shift_e), roll_lanes(rw_ref[at], shift_w)
         )
@@ -353,7 +354,7 @@
                     lane_q,
                     own_ref[f, r],
                     roll_lanes(re_ref[at], 8 - start),
-                    roll_lanes(rw_ref[at], (19 if f == 3 else 18) - start),
+                    roll_lanes(rw_ref[at], (f == 3) if r == last else (24, 18, 12, 7)[f]),
                 )
             )
         for f in range(4):
@@ -803,12 +804,9 @@
             for tr in range(2):
                 for v in range(regs):
                     out[tr, k, pl.ds(v, 8, regs), :] = new[tr][8 * v : 8 * v + 8]
-        for tr in range(2):
-            span = (tr, pl.ds(part * step, step))
-            copies.append(
-                pltpu.make_async_copy(out.at[span], out_hbm.at[span], sems.at[tr, part])
-            )
-            copies[-1].start()
+        span = (slice(None), pl.ds(part * step, step))
+        copies.append(pltpu.make_async_copy(out.at[span], out_hbm.at[span], sems.at[part]))
+        copies[-1].start()
     for copy in copies:
         copy.wait()
 
@@ -921,7 +919,7 @@
     with jax.named_scope("finish"):
         return call(
             finish_kernel, slabs(2, levels),
-            [work(2, levels), pltpu.SemaphoreType.DMA((2, GROUPS))],
+            [work(2, levels), pltpu.SemaphoreType.DMA((GROUPS,))],
             (y, a_end, b_end, own, m2, m3, m1, both), 10**6, 6 * levels * slab, 16,
             out_specs=HBM,
         )

time: 33.8 us -> 33.7 us (level)
  no operation moved by 1% of the time
where the time goes in v3:
time: 33.7 us; the launch traced here: 33.6 us
  Pallas kernels  16.2 us (48%)
  starting transfers between devices  12.8 us (38%)
  waiting for transfers between devices  3.67 us (11%)
  local copies, waits for them, and re-layouts  0.77 us (2%)
    pallas_call x10, Pallas kernels, call(): pl.pallas_call(body, out_shape=out_shape, in_specs=in_specs or [VMEM] * l...  16.2 us
    ppermute x1, waiting for transfers between devices, per_device(): both = lax.ppermute(both, 'dep', swap)  3.64 us
    ppermute x1, starting transfers between devices, per_device(): r_east = lax.ppermute(ww, 'lon', west)  3.39 us
    ppermute x1, starting transfers between devices, per_device(): first = lax.ppermute(first, 'dep', swap)  3.14 us
    ppermute x1, starting transfers between devices, per_device(): pair = lax.ppermute(msg, 'dep', swap)  1.64 us
    ppermute x1, starting transfers between devices, per_device(): m3 = lax.ppermute(m3, 'dep', [(i, i ^ 3) for i in range(dep_n)])  1.51 us
    ppermute x1, starting transfers between devices, per_device(): m1 = lax.ppermute(m1, 'dep', swap)  1.03 us
    ppermute x1, starting transfers between devices, per_device(): m2 = lax.ppermute(m2, 'dep', [(i, i ^ 2) for i in range(dep_n)])  1.02 us
  transfers between devices with their start and end apart: 9, of which 1 were waited for; matrix products, arithmetic and copies ran while one was open for 0% of the time, Pallas kernels for 27%

profile of v3, /device:TPU:0, one launch (start us, length us, event | category | flops | bytes accessed | tf_op | source)
XLA Modules:
  0.0 33.6 jit_solution(5088051268303171114)
XLA Ops:
  0.0 0.0 copy-start.1
  0.0 0.8 %copy-done.1 = s32[64,128]{1,0:T(8,128)S(1)} copy-done((s32[64,128]{1,0:T(8,128)S(1)}, s32[64,128]{1,0:T(8,128)}, u32[]{:S(2)}) %copy-start.1) | copy-done | bytes 32792
  0.8 0.0 copy-start.2
  0.8 3.0 %pack.1 = (f32[5,64,128]{2,1,0:T(8,128)S(1)}, f32[5,64,128]{2,1,0:T(8,128)S(1)}, f32[64,128]{1,0:T(8,128)S(1)}, f32[4,64,128]{2,1,0:T(8,128)S(1)}, f32[4,64,128]...) custom-call(f32[2,20,64,128]{3,2,1,0:T(8,128)} %t_hbm.1, ...), custom_call_target="tpu_custom_call" | custom-call | flops 1000000 | bytes 3932160 | tf_op jit(solution)/shard_map/pack/pallas_call | solution.py:55
  3.8 3.4 %collective-permute-start = (f32[4,64,128]{2,1,0:T(8,128)S(1)}, f32[4,64,128]{2,1,0:T(8,128)S(1)}, u32[]{:S(2)}, u32[]{:S(2)}) collective-permute-start(f32[4,64,128]{2,1,0:T(8,128)S(1)} %get-tuple-element.53), channel_id=1, source_target_pairs={{4,0},{8,4},{12,8},{16,12},{20,16},{24,20},{28,24},{0,28},{5,1},{9... | collective-permute-start | bytes 393224 | tf_op jit(solution)/shard_map/lon_halo/ppermute | solution.py:837
  7.1 0.0 collective-permute-start.1
  7.1 0.0 copy-done.2
  7.1 0.4 %factor.1 = (f32[20,64,128]{2,1,0:T(8,128)S(1)}, f32[20,64,128]{2,1,0:T(8,128)S(1)}, f32[20,64,128]{2,1,0:T(8,128)S(1)}, f32[20,64,128]{2,1,0:T(8,128)S(1)}, f32...) custom-call(f32[20,64,128]{2,1,0:T(8,128)S(1)} %copy-done.2, ...), custom_call_target="tpu_custom_call" | custom-call | flops 10000000 | bytes 3932160 | tf_op jit(solution)/shard_map/factor/pallas_call | solution.py:55
  7.5 1.6 %collective-permute-start.2 = (f32[3,64,128]{2,1,0:T(8,128)S(1)}, f32[3,64,128]{2,1,0:T(8,128)S(1)}, u32[]{:S(2)}, u32[]{:S(2)}) collective-permute-start(f32[3,64,128]{2,1,0:T(8,128)S(1)} %get-tuple-element.55), channel_id=1, source_target_pairs={{0,1},{1,0},{2,3},{3,2},{4,5},{5,4},{6,7},{7,6},{8,9},{9,8},{10,11... | collective-permute-start | bytes 294920 | tf_op jit(solution)/shard_map/pair_coefficients/ppermute | solution.py:846
  9.2 0.3 own_strips.1
  9.5 1.7 %advect_south.1.south_half = f32[2,10,64,128]{3,2,1,0:T(8,128)S(1)} custom-call(f32[20,64,128]{2,1,0:T(8,128)S(1)} %get-tuple-element.42.t0_ref, f32[20,64,128]{2,1,0:T(8,128)S(1)} %get-tuple-element.43.t1_ref, f32[20,64,128]{2,1,0:T(8,128)S(1)} %get-tuple-element.44.u_ref, f32[20,64,128]{2,1,0:T(8,128)S(1)} %get-tuple-element.45.v_ref, ...), custom_call_target="tpu_custom_call" | custom-call | flops 10000000 | bytes 2621440 | tf_op jit(solution)/shard_map/advect_south/pallas_call | solution.py:55
  11.2 0.0 copy-start
  11.2 1.7 %advect_north.1.north_half = f32[2,10,64,128]{3,2,1,0:T(8,128)S(1)} custom-call(f32[20,64,128]{2,1,0:T(8,128)S(1)} %get-tuple-element.42.t0_ref, f32[20,64,128]{2,1,0:T(8,128)S(1)} %get-tuple-element.43.t1_ref, f32[20,64,128]{2,1,0:T(8,128)S(1)} %get-tuple-element.44.u_ref, f32[20,64,128]{2,1,0:T(8,128)S(1)} %get-tuple-element.45.v_ref, ...), custom_call_target="tpu_custom_call" | custom-call | flops 10000000 | bytes 2621440 | tf_op jit(solution)/shard_map/advect_north/pallas_call | solution.py:55
  12.9 0.0 collective-permute-done.2.pair_ref
  12.9 0.0 collective-permute-done.re_ref
  12.9 0.0 collective-permute-done.1.rw_ref
  12.9 0.0 copy-done
  12.9 1.6 %advect_edge.1 = (f32[2,5,64,128]{3,2,1,0:T(8,128)S(1)}, f32[5,64,128]{2,1,0:T(8,128)S(1)}, f32[64,128]{1,0:T(8,128)S(1)}, f32[64,128]{1,0:T(8,128)S(1)}, f32[27...) custom-call(f32[4,5,64,128]{3,2,1,0:T(8,128)S(1)} %get-tuple-element.51.own_ref, ...), custom_call_target="tpu_custom_call" | custom-call | flops 1000000 | bytes 1966080 | tf_op jit(solution)/shard_map/advect_edge/pallas_call | solution.py:55
  14.6 0.1 collective-permute-start.4
  14.6 3.1 %collective-permute-start.3 = (f32[272,128]{1,0:T(8,128)S(1)}, f32[272,128]{1,0:T(8,128)S(1)}, u32[]{:S(2)}, u32[]{:S(2)}) collective-permute-start(f32[272,128]{1,0:T(8,128)S(1)} %get-tuple-element.65), channel_id=1, source_target_pairs={{0,1},{1,0},{2,3},{3,2},{4,5},{5,4},{6,7},{7,6},{8,9},{9,8},{10,11... | collective-permute-start | bytes 417800 | tf_op jit(solution)/shard_map/dep_halo/ppermute | solution.py:888
  17.8 2.4 %patch.1 = (f32[2,20,64,128]{3,2,1,0:T(8,128)S(1)}, f32[2,20,64,128]{3,2,1,0:T(8,128)S(1)}, f32[2,5,64,128]{3,2,1,0:T(8,128)S(1)}) custom-call(f32[2,10,64,128]{3,2,1,0:T(8,128)S(1)} %advect_north.1.north_half, f32[2,10,64,128]{3,2,1,0:T(8,128)S(1)} %advect_south.1.south_half, f32[2,5,64,128]{3,2,1,0:T(8,128)S(1)} %get-tuple-element.56.ea_ref, ...), custom_call_target="tpu_custom_call" | custom-call | flops 10000000 | bytes 5242880 | tf_op jit(solution)/shard_map/patch/pallas_call | solution.py:55
  20.2 2.5 %fluxes.1 = (f32[2,20,64,128]{3,2,1,0:T(8,128)S(1)}, f32[2,20,64,128]{3,2,1,0:T(8,128)S(1)}) custom-call(f32[2,20,64,128]{3,2,1,0:T(8,128)S(1)} %get-tuple-element.59.full_ref, f32[2,20,64,128]{3,2,1,0:T(8,128)S(1)} %get-tuple-element.60.gx_ref, f32[2,5,64,128]{3,2,1,0:T(8,128)S(1)} %get-tuple-element.61.efx_ref, f32[64,128]{1,0:T(8,128)S(1)} %get-tuple-element.62.bmx_ref, ...), custom_call_target="tpu_custom_call" | custom-call | flops 10000000 | bytes 6553600 | tf_op jit(solution)/shard_map/fluxes/pallas_call | solution.py:55
  22.7 0.0 collective-permute-done.3.first_ref
  22.7 0.0 collective-permute-done.4.second_ref
  22.8 1.4 %solve.1 = (f32[2,20,64,128]{3,2,1,0:T(8,128)S(1)}, f32[2,64,128]{2,1,0:T(8,128)S(1)}, f32[2,64,128]{2,1,0:T(8,128)S(1)}, f32[2,64,128]{2,1,0:T(8,128)S(1)}, f32...) custom-call(f32[2,20,64,128]{3,2,1,0:T(8,128)S(1)} %get-tuple-element.59.full_ref, ...), custom_call_target="tpu_custom_call" | custom-call | flops 10000000 | bytes 7864320 | tf_op jit(solution)/shard_map/solve/pallas_call | solution.py:55
  24.1 1.0 %collective-permute-start.5 = (f32[2,64,128]{2,1,0:T(8,128)S(1)}, f32[2,64,128]{2,1,0:T(8,128)S(1)}, u32[]{:S(2)}, u32[]{:S(2)}) collective-permute-start(f32[2,64,128]{2,1,0:T(8,128)S(1)} %get-tuple-element.75), channel_id=1, source_target_pairs={{0,2},{1,3},{2,0},{3,1},{4,6},{5,7},{6,4},{7,5},{8,10},{9,11},{10,... | collective-permute-start | bytes 196616 | tf_op jit(solution)/shard_map/interfaces/ppermute | solution.py:915
  25.2 1.5 %collective-permute-start.6 = (f32[2,64,128]{2,1,0:T(8,128)S(1)}, f32[2,64,128]{2,1,0:T(8,128)S(1)}, u32[]{:S(2)}, u32[]{:S(2)}) collective-permute-start(f32[2,64,128]{2,1,0:T(8,128)S(1)} %get-tuple-element.76), channel_id=1, source_target_pairs={{0,3},{1,2},{2,1},{3,0},{4,7},{5,6},{6,5},{7,4},{8,11},{9,10},{10,... | collective-permute-start | bytes 196616 | tf_op jit(solution)/shard_map/interfaces/ppermute | solution.py:916
  26.7 1.0 %collective-permute-start.7 = (f32[2,64,128]{2,1,0:T(8,128)S(1)}, f32[2,64,128]{2,1,0:T(8,128)S(1)}, u32[]{:S(2)}, u32[]{:S(2)}) collective-permute-start(f32[2,64,128]{2,1,0:T(8,128)S(1)} %get-tuple-element.77), channel_id=1, source_target_pairs={{0,1},{1,0},{2,3},{3,2},{4,5},{5,4},{6,7},{7,6},{8,9},{9,8},{10,11... | collective-permute-start | bytes 196616 | tf_op jit(solution)/shard_map/interfaces/ppermute | solution.py:917
  27.7 1.0 %collective-permute-start.8 = (f32[64,128]{1,0:T(8,128)S(1)}, f32[64,128]{1,0:T(8,128)S(1)}, u32[]{:S(2)}, u32[]{:S(2)}) collective-permute-start(f32[64,128]{1,0:T(8,128)S(1)} %get-tuple-element.78), channel_id=1, source_target_pairs={{0,1},{1,0},{2,3},{3,2},{4,5},{5,4},{6,7},{7,6},{8,9},{9,8},{10,11... | collective-permute-start | bytes 98312 | tf_op jit(solution)/shard_map/interfaces/ppermute | solution.py:918
  28.7 3.6 %collective-permute-done.8.both_ref = f32[64,128]{1,0:T(8,128)S(1)} collective-permute-done((f32[64,128]{1,0:T(8,128)S(1)}, f32[64,128]{1,0:T(8,128)S(1)}, u32[]{:S(2)}, u32[]{:S(2)}) %collective-permute-start.8) | collective-permute-done | bytes 32800 | tf_op jit(solution)/shard_map/interfaces/ppermute | solution.py:918
  32.3 0.0 collective-permute-done.5.r2_ref
  32.3 0.0 collective-permute-done.6.r3_ref
  32.3 0.0 collective-permute-done.7.r1_ref
  32.3 1.2 %finish.1 = f32[2,20,64,128]{3,2,1,0:T(8,128)} custom-call(f32[2,20,64,128]{3,2,1,0:T(8,128)S(1)} %get-tuple-element.71.y_ref, f32[20,64,128]{2,1,0:T(8,128)S(1)} %get-tuple-element.72.a_ref, f32[20,64,128]{2,1,0:T(8,128)S(1)} %get-tuple-element.73.bb_ref, f32[3,64,128]{2,1,0:T(8,128)S(1)} %get-tuple-element.74.own_ref, ...), custom_call_target="tpu_custom_call" | custom-call | flops 1000000 | bytes 3932160 | tf_op jit(solution)/shard_map/finish/pallas_call | solution.py:55
Async XLA Ops:
  0.0 0.8 %copy-start.1 = (s32[64,128]{1,0:T(8,128)S(1)}, s32[64,128]{1,0:T(8,128)}, u32[]{:S(2)}) copy-start(s32[64,128]{1,0:T(8,128)} %b_ref.11) | copy-start | bytes 98308
  0.8 6.4 %copy-start.2 = (f32[20,64,128]{2,1,0:T(8,128)S(1)}, f32[20,64,128]{2,1,0:T(8,128)}, u32[]{:S(2)}) copy-start(f32[20,64,128]{2,1,0:T(8,128)} %kv_ref.1) | copy-start | bytes 1966084
  3.8 9.2 %collective-permute-start = (f32[4,64,128]{2,1,0:T(8,128)S(1)}, f32[4,64,128]{2,1,0:T(8,128)S(1)}, u32[]{:S(2)}, u32[]{:S(2)}) collective-permute-start(f32[4,64,128]{2,1,0:T(8,128)S(1)} %get-tuple-element.53), channel_id=1, source_target_pairs={{4,0},{8,4},{12,8},{16,12},{20,16},{24,20},{28,24},{0,28},{5,1},{9... | collective-permute-start | bytes 393224 | tf_op jit(solution)/shard_map/lon_halo/ppermute | solution.py:837
  7.1 5.8 %collective-permute-start.1 = (f32[4,64,128]{2,1,0:T(8,128)S(1)}, f32[4,64,128]{2,1,0:T(8,128)S(1)}, u32[]{:S(2)}, u32[]{:S(2)}) collective-permute-start(f32[4,64,128]{2,1,0:T(8,128)S(1)} %get-tuple-element.54), channel_id=1, source_target_pairs={{0,4},{4,8},{8,12},{12,16},{16,20},{20,24},{24,28},{28,0},{1,5},{5... | collective-permute-start | bytes 393224 | tf_op jit(solution)/shard_map/lon_halo/ppermute | solution.py:838
  7.5 5.4 %collective-permute-start.2 = (f32[3,64,128]{2,1,0:T(8,128)S(1)}, f32[3,64,128]{2,1,0:T(8,128)S(1)}, u32[]{:S(2)}, u32[]{:S(2)}) collective-permute-start(f32[3,64,128]{2,1,0:T(8,128)S(1)} %get-tuple-element.55), channel_id=1, source_target_pairs={{0,1},{1,0},{2,3},{3,2},{4,5},{5,4},{6,7},{7,6},{8,9},{9,8},{10,11... | collective-permute-start | bytes 294920 | tf_op jit(solution)/shard_map/pair_coefficients/ppermute | solution.py:846
  11.2 1.7 %copy-start = (f32[20,64,128]{2,1,0:T(8,128)S(1)}, f32[20,64,128]{2,1,0:T(8,128)}, u32[]{:S(2)}) copy-start(f32[20,64,128]{2,1,0:T(8,128)} %kh_ref.5) | copy-start | bytes 1966084
  14.6 8.2 %collective-permute-start.4 = (f32[400,128]{1,0:T(8,128)S(1)}, f32[400,128]{1,0:T(8,128)S(1)}, u32[]{:S(2)}, u32[]{:S(2)}) collective-permute-start(f32[400,128]{1,0:T(8,128)S(1)} %get-tuple-element.66), channel_id=1, source_target_pairs={{0,4},{1,2},{2,1},{3,7},{4,0},{5,6},{6,5},{7,3},{8,12},{9,10},{10,... | collective-permute-start | bytes 614408 | tf_op jit(solution)/shard_map/dep_halo/ppermute | solution.py:889
  14.6 8.1 %collective-permute-start.3 = (f32[272,128]{1,0:T(8,128)S(1)}, f32[272,128]{1,0:T(8,128)S(1)}, u32[]{:S(2)}, u32[]{:S(2)}) collective-permute-start(f32[272,128]{1,0:T(8,128)S(1)} %get-tuple-element.65), channel_id=1, source_target_pairs={{0,1},{1,0},{2,3},{3,2},{4,5},{5,4},{6,7},{7,6},{8,9},{9,8},{10,11... | collective-permute-start | bytes 417800 | tf_op jit(solution)/shard_map/dep_halo/ppermute | solution.py:888
  24.1 8.2 %collective-permute-start.5 = (f32[2,64,128]{2,1,0:T(8,128)S(1)}, f32[2,64,128]{2,1,0:T(8,128)S(1)}, u32[]{:S(2)}, u32[]{:S(2)}) collective-permute-start(f32[2,64,128]{2,1,0:T(8,128)S(1)} %get-tuple-element.75), channel_id=1, source_target_pairs={{0,2},{1,3},{2,0},{3,1},{4,6},{5,7},{6,4},{7,5},{8,10},{9,11},{10,... | collective-permute-start | bytes 196616 | tf_op jit(solution)/shard_map/interfaces/ppermute | solution.py:915
  25.2 7.2 %collective-permute-start.6 = (f32[2,64,128]{2,1,0:T(8,128)S(1)}, f32[2,64,128]{2,1,0:T(8,128)S(1)}, u32[]{:S(2)}, u32[]{:S(2)}) collective-permute-start(f32[2,64,128]{2,1,0:T(8,128)S(1)} %get-tuple-element.76), channel_id=1, source_target_pairs={{0,3},{1,2},{2,1},{3,0},{4,7},{5,6},{6,5},{7,4},{8,11},{9,10},{10,... | collective-permute-start | bytes 196616 | tf_op jit(solution)/shard_map/interfaces/ppermute | solution.py:916
  26.7 5.7 %collective-permute-start.7 = (f32[2,64,128]{2,1,0:T(8,128)S(1)}, f32[2,64,128]{2,1,0:T(8,128)S(1)}, u32[]{:S(2)}, u32[]{:S(2)}) collective-permute-start(f32[2,64,128]{2,1,0:T(8,128)S(1)} %get-tuple-element.77), channel_id=1, source_target_pairs={{0,1},{1,0},{2,3},{3,2},{4,5},{5,4},{6,7},{7,6},{8,9},{9,8},{10,11... | collective-permute-start | bytes 196616 | tf_op jit(solution)/shard_map/interfaces/ppermute | solution.py:917
  27.7 4.6 %collective-permute-start.8 = (f32[64,128]{1,0:T(8,128)S(1)}, f32[64,128]{1,0:T(8,128)S(1)}, u32[]{:S(2)}, u32[]{:S(2)}) collective-permute-start(f32[64,128]{1,0:T(8,128)S(1)} %get-tuple-element.78), channel_id=1, source_target_pairs={{0,1},{1,0},{2,3},{3,2},{4,5},{5,4},{6,7},{7,6},{8,9},{9,8},{10,11... | collective-permute-start | bytes 98312 | tf_op jit(solution)/shard_map/interfaces/ppermute | solution.py:918
